TPU v7x, 128 devices: a whole 4x4x4 slice. The times are simulated.
128 devices in a mesh: dp: 4 (over z), mem: 32 (over x, y, core).
Axes of the slice: x: 4, y: 4, z: 4, core: 2. Of those that a mesh axis runs over, the one named last changes fastest.
Arguments:
- queries: bfloat16 [8192, 2048], P('dp'), may hold values from -9 to 9
- grad_out: bfloat16 [8192, 2048], P('dp'), may hold values from -192 to 192
- mem_keys: bfloat16 [16384, 2048], P('mem'), may hold values from -4 to 4
- mem_values: bfloat16 [16384, 2048], P('mem'), may hold values from -6 to 6
- block_lists: int32 [64, 16], P('dp'), may hold values from 0 to 127, all different within a row
- block_home: int32 [128], replicated, may hold values from 0 to 127, each once
Outputs:
- grad_queries: bfloat16 [8192, 2048], P(('dp', 'mem'))
- grad_keys: bfloat16 [16384, 2048], P('mem')
- grad_values: bfloat16 [16384, 2048], P('mem')
Inputs may be any that keep to these rules, and one draw needn't show every extreme that they name: `block_lists`: each row names 16 different memory blocks; every block is named by some row, some blocks far more often than others. `block_home`: each stored block holds exactly one memory block; stored block j lies on index j // 4 of mem.
All inputs are finite; a program needn't handle non-finite values.
Results may differ from a plain program's by a relative error of at most 0.0085.
Values may be sent and summed in bfloat16 or wider, within the bound.
No kernel may reach another device: no remote copies, remote signals or barrier semaphores. Data moves between devices by JAX's collectives and lax.ppermute only.
A program may use at most 192 MiB of HBM per device.

v0:
```python
import functools

import jax
import jax.numpy as jnp
from jax import lax
from jax.experimental import pallas as pl
from jax.experimental.pallas import tpu as pltpu
from jax.sharding import PartitionSpec as P

H = 16
DH = 128
BLK = 128
TOPB = 16
NZ = 4
NCHIP = 16
QPER = 8
NQ = NZ * QPER
NB = 2 * NCHIP
NENT = NQ * TOPB
EARLY = (0, 1, 3)
LATE = (2,)
LATE_AT = len(EARLY) * QPER * TOPB + 8
COUNT = LATE_AT + len(LATE) * QPER * TOPB + 16
NCOPY = 2 * NZ + 2
CHUNKS = 4
UNROLL_F = 8
UNROLL_B = 16
SCALE = DH ** (-0.5)
BF = jnp.bfloat16
F32 = jnp.float32
MB = 1 << 20


NT = (((1,), (1,)), ((), ()))
NN = (((1,), (0,)), ((), ()))
TN = (((0,), (0,)), ((), ()))


def position():
    m = lax.axis_index("mem")
    return lax.axis_index("dp"), m >> 1, m & 1


def dot(a, b, dims):
    return lax.dot_general(a, b, dims, preferred_element_type=F32)


def over_z(array, shift):
    return lax.ppermute(array, "dp", [(i, (i + shift) % NZ) for i in range(NZ)])


def swap_cores(array):
    return lax.ppermute(array, "mem", [(i, i ^ 1) for i in range(2 * NCHIP)])


def plane_exchange(array):
    groups = [[2 * c + k for c in range(NCHIP)] for k in range(2)]
    return lax.all_to_all(array, "mem", 0, 0, axis_index_groups=groups)


def prepare_kernel(queries, grads, keys, values, q, g, kv, sems):
    z, c, k = position()
    cols = pl.ds(pl.multiple_of(c * DH, DH), DH)
    pairs = []
    for i in range(QPER):
        rows = pl.ds(pl.multiple_of((k * QPER + i) * BLK, BLK), BLK)
        pairs.append((queries.at[rows, cols], q.at[i]))
        pairs.append((grads.at[rows, cols], g.at[i]))
    rows = pl.ds(pl.multiple_of(z * BLK, BLK), BLK)
    for h in range(H):
        cols = slice(h * DH, (h + 1) * DH)
        pairs.append((keys.at[rows, cols], kv.at[h, :BLK]))
        pairs.append((values.at[rows, cols], kv.at[h, BLK:]))
    copies = [pltpu.make_async_copy(a, b, sems.at[n]) for n, (a, b) in enumerate(pairs)]
    for copy in copies:
        copy.start()
    for copy in copies:
        copy.wait()


def prepare(queries, grads, keys, values):
    vmem = pl.BlockSpec(memory_space=pltpu.VMEM)
    far = pl.BlockSpec(memory_space=pl.ANY)
    return pl.pallas_call(
        prepare_kernel,
        out_shape=(
            jax.ShapeDtypeStruct((QPER, BLK, DH), BF),
            jax.ShapeDtypeStruct((QPER, BLK, DH), BF),
            jax.ShapeDtypeStruct((H, 2 * BLK, DH), BF),
        ),
        in_specs=[far] * 4,
        out_specs=(vmem, vmem, vmem),
        scratch_shapes=[pltpu.SemaphoreType.DMA((2 * QPER + 2 * H,))],
        compiler_params=pltpu.CompilerParams(vmem_limit_bytes=60 * MB),
        name="prepare",
    )(queries, grads, keys, values)


def list_kernel(l0, l1, l2, l3, home, ents):
    z, _, k = position()

    def group(r, lists, n):
        def block(i, n):
            q = r * QPER + i
            seen = jnp.int32(0)
            for t in range(TOPB):
                slot = home[lists[k * QPER + i, t]]
                mine = (slot & 3) == z
                owner = slot >> 2
                b = ((owner & 1) ^ k) * NCHIP + (owner >> 1)
                ents[n] = (q << 15) | ((seen * NQ + q) << 5) | b
                step = mine.astype(jnp.int32)
                n = n + step
                seen = seen + step
            return n

        return lax.fori_loop(0, QPER, block, n)

    every = (l0, l1, l2, l3)
    for part, (start, groups) in enumerate(((0, EARLY), (LATE_AT, LATE))):
        n = jnp.int32(start)
        for r in groups:
            n = group(r, every[r], n)
        for u in range(8 if start == 0 else 16):
            ents[n + u] = ((NQ + groups[0] * QPER) << 15) | (NENT << 5)
        ents[COUNT + part] = n - start


def make_list(lists, home):
    smem = pl.BlockSpec(memory_space=pltpu.SMEM)
    return pl.pallas_call(
        list_kernel,
        out_shape=jax.ShapeDtypeStruct((COUNT + 8,), jnp.int32),
        in_specs=[smem] * 5,
        out_specs=smem,
        compiler_params=pltpu.CompilerParams(vmem_limit_bytes=MB),
        name="entry_list",
    )(*lists, home)


def fetch(groups, qrefs, grefs, kvrefs, qs, gs, kv, sems):
    pairs = [(ref, kv.at[p]) for p, ref in enumerate(kvrefs)]
    pairs += [(ref, qs.at[r]) for r, ref in zip(groups, qrefs)]
    pairs += [(ref, gs.at[r]) for r, ref in zip(groups, grefs)]
    copies = [pltpu.make_async_copy(a, b, sems.at[n]) for n, (a, b) in enumerate(pairs)]
    for copy in copies:
        copy.start()
    return copies


def unpack(p):
    q = p >> 15
    b = p & 31
    return (q >> 3) & 3, q & 7, q, (p >> 5) & 1023, b >> 4, b & 15


def fwd_kernel(groups, start, ents, before, *refs):
    size = len(groups)
    out, qs, gs, kv, st, sems = refs[2 * size + 2 :]
    copies = fetch(
        groups, refs[:size], refs[size : 2 * size], refs[2 * size : 2 * size + 2], qs, gs, kv, sems
    )
    st[0] = jnp.full((NENT + 8, DH), -1e30, F32)
    st[1] = jnp.zeros((NENT + 8, DH), F32)
    st[2] = jnp.zeros((NENT + 8, DH), F32)
    for copy in copies:
        copy.wait()

    def body(n, carry):
        parts = [unpack(ents[start + UNROLL_F * n + u]) for u in range(UNROLL_F)]
        scores = [dot(kv[p[4], p[5], :BLK], qs[p[0], p[1]], NT) * SCALE for p in parts]
        dprob = [dot(kv[p[4], p[5], BLK:], gs[p[0], p[1]], NT) for p in parts]
        highs = [jnp.max(x, axis=0, keepdims=True) for x in scores]
        expo = [jnp.exp(x - high) for x, high in zip(scores, highs)]
        for p, high, e, d in zip(parts, highs, expo, dprob):
            row = pl.ds(p[3], 1)
            st[0, row, :] = high
            st[1, row, :] = jnp.sum(e, axis=0, keepdims=True)
            st[2, row, :] = jnp.sum(e.astype(BF).astype(F32) * d, axis=0, keepdims=True)
        return carry

    part = 0 if start == 0 else 1
    lax.fori_loop(0, (ents[COUNT + part] + UNROLL_F - 1) // UNROLL_F, body, 0)
    out[...] = before[...]
    for r in groups:
        rows = [slice(e * NQ + r * QPER, e * NQ + (r + 1) * QPER) for e in range(TOPB)]
        high = st[0, rows[0]]
        for row in rows[1:]:
            high = jnp.maximum(high, st[0, row])
        total = jnp.zeros((QPER, DH), F32)
        prod = jnp.zeros((QPER, DH), F32)
        for row in rows:
            weight = jnp.exp(st[0, row] - high)
            total = total + weight * st[1, row]
            prod = prod + weight * st[2, row]
        at = slice(r * QPER, (r + 1) * QPER)
        out[0, at] = high
        out[1, at] = total
        out[2, at] = prod


def scratch_in():
    return [
        pltpu.VMEM((NZ, QPER, BLK, DH), BF),
        pltpu.VMEM((NZ, QPER, BLK, DH), BF),
        pltpu.VMEM((2, NCHIP, 2 * BLK, DH), BF),
    ]


def forward(groups, start, ents, before, qparts, gparts, kvs):
    smem = pl.BlockSpec(memory_space=pltpu.SMEM)
    vmem = pl.BlockSpec(memory_space=pltpu.VMEM)
    far = pl.BlockSpec(memory_space=pl.ANY)
    return pl.pallas_call(
        functools.partial(fwd_kernel, groups, start),
        out_shape=jax.ShapeDtypeStruct((3, NQ, DH), F32),
        in_specs=[smem, vmem] + [far] * (2 * len(groups) + 2),
        out_specs=vmem,
        scratch_shapes=scratch_in()
        + [pltpu.VMEM((3, NENT + 8, DH), F32), pltpu.SemaphoreType.DMA((NCOPY,))],
        compiler_params=pltpu.CompilerParams(vmem_limit_bytes=14 * MB),
        name="forward",
    )(ents, before, *qparts, *gparts, *kvs)


def bwd_kernel(
    ents, s0, s1, s2, s3, q0, q1, q2, q3, g0, g1, g2, g3, kva, kvb,
    dq0, dq1, dq2, dq3, own, other,
    qs, gs, kv, dq, dkv, away, dqs, lse, delta, sems, outsems,
):
    copies = fetch(range(NZ), (q0, q1, q2, q3), (g0, g1, g2, g3), (kva, kvb), qs, gs, kv, sems)

    def clear(i, carry):
        zero = jnp.zeros((BLK, DH), F32)
        dq[i] = zero
        dkv[i, :BLK] = zero
        dkv[i, BLK:] = zero
        return carry

    lax.fori_loop(0, NQ, clear, 0)
    for r in range(NZ):
        rows = slice(r * QPER, (r + 1) * QPER)
        parts = []
        for ref, shift in ((s0, 0), (s1, 1), (s2, 2), (s3, 3)):
            at = (r + shift) % NZ
            parts.append([ref[n, at * QPER : (at + 1) * QPER] for n in range(3)])
        high = jnp.maximum(
            jnp.maximum(parts[0][0], parts[1][0]), jnp.maximum(parts[2][0], parts[3][0])
        )
        total = jnp.zeros((QPER, DH), F32)
        prod = jnp.zeros((QPER, DH), F32)
        for part in parts:
            weight = jnp.exp(part[0] - high)
            total = total + weight * part[1]
            prod = prod + weight * part[2]
        lse[rows] = high + jnp.log(total)
        delta[rows] = prod / total
    for copy in copies:
        copy.wait()

    lse[NQ:] = jnp.full((NQ, DH), 1e30, F32)
    delta[NQ:] = jnp.zeros((NQ, DH), F32)

    early = ents[COUNT]
    steps = (early + ents[COUNT + 1] + UNROLL_B - 1) // UNROLL_B

    def body(n, carry):
        parts = []
        for u in range(UNROLL_B):
            at = n * UNROLL_B + u
            parts.append(unpack(ents[jnp.where(at < early, at, at + (LATE_AT - early))]))
        keys = [kv[p[4], p[5], :BLK] for p in parts]
        quer = [qs[p[0], p[1]] for p in parts]
        grad = [gs[p[0], p[1]] for p in parts]
        scores = [dot(a, b, NT) * SCALE for a, b in zip(keys, quer)]
        dprob = [dot(kv[p[4], p[5], BLK:], b, NT) for p, b in zip(parts, grad)]
        probs = [jnp.exp(x - lse[pl.ds(p[2], 1), :]) for x, p in zip(scores, parts)]
        dscore = [
            (x * (d - delta[pl.ds(p[2], 1), :]) * SCALE).astype(BF)
            for x, d, p in zip(probs, dprob, parts)
        ]
        gv = [dot(x.astype(BF), b, NN) for x, b in zip(probs, grad)]
        gk = [dot(x, b, NN) for x, b in zip(dscore, quer)]
        gq = [dot(x, b, TN) for x, b in zip(dscore, keys)]
        for p, a, b, c in zip(parts, gv, gk, gq):
            at = p[4] * NCHIP + p[5]
            dkv[at, BLK:] += a
            dkv[at, :BLK] += b
            dq[p[0] * QPER + p[1]] += c
        return carry

    lax.fori_loop(0, steps, body, 0)
    sends = []
    for n, ref in ((1, other), (0, own)):
        half = slice(n * NCHIP, (n + 1) * NCHIP)
        away[half] = dkv[half].astype(BF)
        sends.append(pltpu.make_async_copy(away.at[half], ref, outsems.at[n]))
        sends[-1].start()
    for r, ref in enumerate((dq0, dq1, dq2, dq3)):
        part = slice(r * QPER, (r + 1) * QPER)
        dqs[part] = dq[part].astype(BF)
        sends.append(pltpu.make_async_copy(dqs.at[part], ref, outsems.at[2 + r]))
        sends[-1].start()
    for send in sends:
        send.wait()


def backward(ents, stats, xparts, kvs):
    smem = pl.BlockSpec(memory_space=pltpu.SMEM)
    vmem = pl.BlockSpec(memory_space=pltpu.VMEM)
    far = pl.BlockSpec(memory_space=pl.ANY)
    tile = (BLK, DH)
    outs = [jax.ShapeDtypeStruct((QPER,) + tile, BF)] * 4
    pair = (NCHIP, 2 * BLK, DH)
    outs += [jax.ShapeDtypeStruct(pair, BF)] * 2
    return pl.pallas_call(
        bwd_kernel,
        out_shape=tuple(outs),
        in_specs=[smem] + [vmem] * 4 + [far] * 10,
        out_specs=tuple([far] * 6),
        scratch_shapes=scratch_in()
        + [
            pltpu.VMEM((NQ,) + tile, F32),
            pltpu.VMEM((NB, 2 * BLK, DH), F32),
            pltpu.VMEM((NB, 2 * BLK, DH), BF),
            pltpu.VMEM((NQ,) + tile, BF),
            pltpu.VMEM((2 * NQ, DH), F32),
            pltpu.VMEM((2 * NQ, DH), F32),
            pltpu.SemaphoreType.DMA((NCOPY,)),
            pltpu.SemaphoreType.DMA((6,)),
        ],
        compiler_params=pltpu.CompilerParams(vmem_limit_bytes=24 * MB),
        name="backward",
    )(ents, *stats, *xparts, *kvs)


def place_parts(z, parts, sems):
    copies = []
    for n, (r, ref, out) in enumerate(parts):
        rows = pl.ds(pl.multiple_of(((z + r) & 3) * BLK, BLK), BLK)
        copies.append(pltpu.make_async_copy(ref, out.at[rows], sems.at[n]))
    for copy in copies:
        copy.start()
    for copy in copies:
        copy.wait()


def near_kernel(k0, k1, k3, v0, v1, v3, outk, outv, sems):
    parts = [(0, k0, outk), (1, k1, outk), (3, k3, outk)]
    parts += [(0, v0, outv), (1, v1, outv), (3, v3, outv)]
    place_parts(position()[0], parts, sems)


def far_kernel(k2, v2, ink, inv, outk, outv, held, insems, outsems):
    z = position()[0]
    rows = BLK // CHUNKS
    came, went = [], []
    for n in range(CHUNKS):
        for t, (ref, out) in enumerate(((k2, outk), (v2, outv))):
            at = pl.ds(n * rows, rows)
            to = pl.ds(pl.multiple_of(((z + 2) & 3) * BLK + n * rows, rows), rows)
            s = 2 * n + t
            came.append(pltpu.make_async_copy(ref.at[at], held.at[t, at], insems.at[s]))
            went.append(pltpu.make_async_copy(held.at[t, at], out.at[to], outsems.at[s]))
    for copy in came:
        copy.start()
    for first, second in zip(came, went):
        first.wait()
        second.start()
    for copy in went:
        copy.wait()


def place_near(kparts, vparts):
    smem = pl.BlockSpec(memory_space=pltpu.SMEM)
    vmem = pl.BlockSpec(memory_space=pltpu.VMEM)
    far = pl.BlockSpec(memory_space=pl.ANY)
    shape = jax.ShapeDtypeStruct((NZ * BLK, H * DH), BF)
    return pl.pallas_call(
        near_kernel,
        out_shape=(shape, shape),
        in_specs=[vmem] * 6,
        out_specs=(far, far),
        scratch_shapes=[pltpu.SemaphoreType.DMA((6,))],
        compiler_params=pltpu.CompilerParams(vmem_limit_bytes=8 * MB),
        name="place_near",
    )(*kparts, *vparts)


def place_far(near, k_far, v_far):
    far = pl.BlockSpec(memory_space=pl.ANY)
    shape = jax.ShapeDtypeStruct((NZ * BLK, H * DH), BF)
    return pl.pallas_call(
        far_kernel,
        out_shape=(shape, shape),
        in_specs=[far] * 4,
        out_specs=(far, far),
        scratch_shapes=[
            pltpu.VMEM((2, BLK, H * DH), BF),
            pltpu.SemaphoreType.DMA((2 * CHUNKS,)),
            pltpu.SemaphoreType.DMA((2 * CHUNKS,)),
        ],
        input_output_aliases={2: 0, 3: 1},
        compiler_params=pltpu.CompilerParams(vmem_limit_bytes=8 * MB),
        name="place_far",
    )(k_far, v_far, *near)


def heads_first(array):
    return jnp.transpose(array.reshape(array.shape[0], H, DH), (1, 0, 2))


def rows_first(array):
    return jnp.transpose(array, (1, 0, 2)).reshape(array.shape[1], H * DH)


def per_device(queries, grad_out, mem_keys, mem_values, block_lists, block_home):
    k = lax.axis_index("mem") & 1
    q_own, g_own, kv_cat = prepare(queries, grad_out, mem_keys, mem_values)
    lists = tuple(over_z(block_lists, shift) for shift in (-1, 2, 1))
    kv_cat, lists = lax.optimization_barrier((kv_cat, lists))
    ents = make_list((block_lists,) + lists, block_home)
    q_prev = over_z(q_own, 1)
    g_next = over_z(g_own, -1)
    g_prev = over_z(g_own, 1)
    q_next = over_z(q_own, -1)
    kv_own, q_prev, g_next, g_prev, q_next, ents = lax.optimization_barrier(
        (plane_exchange(kv_cat), q_prev, g_next, g_prev, q_next, ents)
    )
    q_far = over_z(q_prev, 1)
    g_far = over_z(g_next, -1)
    kvs = (kv_own, swap_cores(kv_own))
    xparts = (q_own, q_next, q_far, q_prev, g_own, g_next, g_far, g_prev)

    stat = jnp.zeros((3, NQ, DH), F32)
    stat = forward(EARLY, 0, ents, stat, (q_own, q_next, q_prev), (g_own, g_next, g_prev), kvs)
    stat = forward(LATE, LATE_AT, ents, stat, (q_far,), (g_far,), kvs)
    stats = (stat, over_z(stat, 1), over_z(stat, 2), over_z(stat, -1))
    dq0, dq1, dq2, dq3, own, other = backward(ents, stats, xparts, kvs)

    both = (own.astype(F32) + swap_cores(other).astype(F32)).astype(BF)
    got = plane_exchange(both)
    k_own, v_own = rows_first(got[:, :BLK]), rows_first(got[:, BLK:])
    v_prev = over_z(v_own, 1)
    v_next = over_z(v_own, -1)
    k_next = over_z(k_own, -1)
    k_prev = over_z(k_own, 1)
    dq_sum = (
        dq0.astype(F32)
        + over_z(dq1, 1).astype(F32)
        + over_z(dq3, -1).astype(F32)
        + over_z(dq2, 2).astype(F32)
    ).astype(BF)
    half = BLK // 2
    keep = lax.dynamic_slice_in_dim(dq_sum, k * half, half, 1)
    give = lax.dynamic_slice_in_dim(dq_sum, (1 - k) * half, half, 1)
    got = swap_cores(give)
    whole = jnp.where(
        k == 0, jnp.concatenate([keep, got], axis=0), jnp.concatenate([got, keep], axis=0)
    )
    whole, v_prev, k_next = lax.optimization_barrier((whole, v_prev, k_next))
    v_far = over_z(v_prev, 1)
    k_far = over_z(k_next, -1)
    near = place_near((k_own, k_next, k_prev), (v_own, v_next, v_prev))
    grad_keys, grad_values = place_far(near, k_far, v_far)
    grad_queries = rows_first(plane_exchange(whole))
    return grad_queries, grad_keys, grad_values


def solution(mesh):
    in_specs = (P("dp", None), P("dp", None), P("mem", None), P("mem", None), P("dp", None), P())
    out_specs = (P(("dp", "mem"), None), P("mem", None), P("mem", None))
    return jax.shard_map(
        per_device, mesh=mesh, in_specs=in_specs, out_specs=out_specs, check_vma=False
    )
```

profile of v0, /device:TPU:0, one launch (start us, length us, event | category | flops | bytes accessed | tf_op | source)
XLA Modules:
  0.0 135.0 jit_solution(13677979744470001277)
XLA Ops:
  0.6 4.0 %collective-permute-start.1 = (s32[16,16]{1,0:T(8,128)}, s32[16,16]{1,0:T(8,128)S(1)}, u32[]{:S(2)}, u32[]{:S(2)}) collective-permute-start(s32[16,16]{1,0:T(8,128)} %l0.1), channel_id=1, source_target_pairs={{0,64},{32,96},{64,0},{96,32},{1,65},{33,97},{65,1},{97,33},{2,66}... | collective-permute-start | bytes 3080 | tf_op jit(solution)/shard_map/ppermute | solution.py:49
  6.7 2.9 %prepare.1 = (bf16[8,128,128]{2,1,0:T(8,128)(2,1)}, bf16[8,128,128]{2,1,0:T(8,128)(2,1)}, bf16[16,256,128]{2,1,0:T(8,128)(2,1)}) custom-call(bf16[2048,2048]{1,0:T(8,128)(2,1)} %queries.1, bf16[2048,2048]{1,0:T(8,128)(2,1)} %grads.1, bf16[512,2048]{1,0:T(8,128)(2,1)} %keys.1, bf16[512,2048]{1,0:T(8,128)(2,1)} %values.1), custom_call_target="tpu_custom_call" | custom-call | tf_op jit(solution)/shard_map/prepare/pallas_call | solution.py:84
  10.5 7.0 %all-to-all-start = ((bf16[16,256,128]{2,1,0:T(8,128)(2,1)}), bf16[16,256,128]{2,1,0:T(8,128)(2,1)S(1)}, u32[]{:S(2)}, u32[]{:S(2)}) async-start(bf16[16,256,128]{2,1,0:T(8,128)(2,1)} %get-tuple-element.30), calls=%async_computation | async-start | bytes 2097152 | tf_op jit(solution)/shard_map/all_to_all | solution.py:58
  20.0 2.8 %collective-permute-start.4 = (bf16[8,128,128]{2,1,0:T(8,128)(2,1)S(1)}, bf16[8,128,128]{2,1,0:T(8,128)(2,1)S(1)}, u32[]{:S(2)}, u32[]{:S(2)}) collective-permute-start(bf16[8,128,128]{2,1,0:T(8,128)(2,1)S(1)} %copy-done.1), channel_id=1, source_target_pairs={{0,96},{32,0},{64,32},{96,64},{1,97},{33,1},{65,33},{97,65},{2,98}... | collective-permute-start | bytes 786440 | tf_op jit(solution)/shard_map/ppermute | solution.py:49
  22.9 4.9 %entry_list.1.ents = s32[544]{0:T(1024)S(1)} custom-call(s32[16,16]{1,0:T(8,128)S(1)} %copy-done.2, s32[16,16]{1,0:T(8,128)S(1)} %collective-permute-done.l1, s32[16,16]{1,0:T(8,128)S(1)} %collective-permute-done.1.l2, s32[16,16]{1,0:T(8,128)S(1)} %collective-permute-done.2.l3, s32[128]{0:T(128)S(1)} %copy-done.3), custom_call_target="tpu_custom_call" | custom-call | tf_op jit(solution)/shard_map/entry_list/pallas_call | solution.py:131
  29.4 3.0 %collective-permute-done.5.refs_5_.g3 = bf16[8,128,128]{2,1,0:T(8,128)(2,1)S(1)} collective-permute-done((bf16[8,128,128]{2,1,0:T(8,128)(2,1)S(1)}, bf16[8,128,128]{2,1,0:T(8,128)(2,1)S(1)}, u32[]{:S(2)}, u32[]{:S(2)}) %collective-permute-start.5) | collective-permute-done | bytes 262176 | tf_op jit(solution)/shard_map/ppermute | solution.py:49
  34.3 2.2 %collective-permute-start.9 = (bf16[8,128,128]{2,1,0:T(8,128)(2,1)S(1)}, bf16[8,128,128]{2,1,0:T(8,128)(2,1)S(1)}, u32[]{:S(2)}, u32[]{:S(2)}) collective-permute-start(bf16[8,128,128]{2,1,0:T(8,128)(2,1)S(1)} %collective-permute-done.4.refs_4_.g1), channel_id=1, source_target_pairs={{0,96},{32,0},{64,32},{96,64},{1,97},{33,1},{65,33},{97,65},{2,98}... | collective-permute-start | bytes 786440 | tf_op jit(solution)/shard_map/ppermute | solution.py:49
  36.4 7.5 %forward.2.before = f32[3,32,128]{2,1,0:T(8,128)S(1)} custom-call(s32[544]{0:T(1024)S(1)} %entry_list.1.ents, f32[3,32,128]{2,1,0:T(8,128)S(1)} %broadcast_in_dim.3.before, bf16[8,128,128]{2,1,0:T(8,128)(2,1)S(1)} %copy-done, bf16[8,128,128]{2,1,0:T(8,128)(2,1)S(1)} %collective-permute-done.6.refs_1_.q1, ...), custom_call_target="tpu_custom_call" | custom-call | tf_op jit(solution)/shard_map/forward/pallas_call | solution.py:214
  44.0 2.9 %forward.3.s0 = f32[3,32,128]{2,1,0:T(8,128)S(1)} custom-call(s32[544]{0:T(1024)S(1)} %entry_list.1.ents, f32[3,32,128]{2,1,0:T(8,128)S(1)} %forward.2.before, bf16[8,128,128]{2,1,0:T(8,128)(2,1)S(1)} %collective-permute-done.8.refs_0_.q2, bf16[8,128,128]{2,1,0:T(8,128)(2,1)S(1)} %collective-permute-done.9.refs_1_.g2, ...), custom_call_target="tpu_custom_call" | custom-call | tf_op jit(solution)/shard_map/forward/pallas_call | solution.py:214
  46.9 2.7 %collective-permute-start.12 = (f32[3,32,128]{2,1,0:T(8,128)S(1)}, f32[3,32,128]{2,1,0:T(8,128)S(1)}, u32[]{:S(2)}, u32[]{:S(2)}) collective-permute-start(f32[3,32,128]{2,1,0:T(8,128)S(1)} %forward.3.s0), channel_id=1, source_target_pairs={{0,96},{32,0},{64,32},{96,64},{1,97},{33,1},{65,33},{97,65},{2,98}... | collective-permute-start | bytes 147464 | tf_op jit(solution)/shard_map/ppermute | solution.py:49
  51.6 3.6 %collective-permute-done.11.s2 = f32[3,32,128]{2,1,0:T(8,128)S(1)} collective-permute-done((f32[3,32,128]{2,1,0:T(8,128)S(1)}, f32[3,32,128]{2,1,0:T(8,128)S(1)}, u32[]{:S(2)}, u32[]{:S(2)}) %collective-permute-start.11) | collective-permute-done | bytes 49184 | tf_op jit(solution)/shard_map/ppermute | solution.py:49
  55.8 13.6 %backward.1 = (bf16[8,128,128]{2,1,0:T(8,128)(2,1)S(1)}, bf16[8,128,128]{2,1,0:T(8,128)(2,1)}, bf16[8,128,128]{2,1,0:T(8,128)(2,1)}, bf16[8,128,128]{2,1,0:T(8,1...) custom-call(s32[544]{0:T(1024)S(1)} %entry_list.1.ents, f32[3,32,128]{2,1,0:T(8,128)S(1)} %forward.3.s0, ...), custom_call_target="tpu_custom_call" | custom-call | tf_op jit(solution)/shard_map/backward/pallas_call | solution.py:316
  69.5 2.6 %collective-permute-done.17 = bf16[16,256,128]{2,1,0:T(8,128)(2,1)S(1)} collective-permute-done((bf16[16,256,128]{2,1,0:T(8,128)(2,1)S(1)}, bf16[16,256,128]{2,1,0:T(8,128)(2,1)S(1)}, u32[]{:S(2)}, u32[]{:S(2)}) %collective-permute-start.17) | collective-permute-done | bytes 1048608 | tf_op jit(solution)/shard_map/ppermute | solution.py:53
  73.4 5.7 %all-to-all-start.1 = ((bf16[16,256,128]{2,1,0:T(8,128)(2,1)}), bf16[16,256,128]{2,1,0:T(8,128)(2,1)S(1)}, u32[]{:S(2)}, u32[]{:S(2)}) async-start(bf16[16,256,128]{2,1,0:T(8,128)(2,1)} %add_convert_fusion), calls=%async_computation.1 | async-start | bytes 2097152 | tf_op jit(solution)/shard_map/all_to_all | solution.py:58
  79.1 2.2 %collective-permute-start.13 = (bf16[8,128,128]{2,1,0:T(8,128)(2,1)}, bf16[8,128,128]{2,1,0:T(8,128)(2,1)S(1)}, u32[]{:S(2)}, u32[]{:S(2)}) collective-permute-start(bf16[8,128,128]{2,1,0:T(8,128)(2,1)} %get-tuple-element.43), channel_id=1, source_target_pairs={{0,32},{32,64},{64,96},{96,0},{1,33},{33,65},{65,97},{97,1},{2,34}... | collective-permute-start | bytes 786440 | tf_op jit(solution)/shard_map/ppermute | solution.py:49
  83.5 13.8 %all-to-all-done.1 = bf16[16,256,128]{2,1,0:T(8,128)(2,1)S(1)} async-done(((bf16[16,256,128]{2,1,0:T(8,128)(2,1)}), bf16[16,256,128]{2,1,0:T(8,128)(2,1)S(1)}, u32[]{:S(2)}, u32[]{:S(2)}) %all-to-all-start.1) | async-done | bytes 1048608 | tf_op jit(solution)/shard_map/all_to_all | solution.py:58
  97.6 2.2 %collective-permute-start.18 = (bf16[128,2048]{1,0:T(8,128)(2,1)S(1)}, bf16[128,2048]{1,0:T(8,128)(2,1)S(1)}, u32[]{:S(2)}, u32[]{:S(2)}) collective-permute-start(bf16[128,2048]{1,0:T(8,128)(2,1)S(1)} %bitcast.21), channel_id=1, source_target_pairs={{0,32},{32,64},{64,96},{96,0},{1,33},{33,65},{65,97},{97,1},{2,34}... | collective-permute-start | bytes 1572872 | tf_op jit(solution)/shard_map/ppermute | solution.py:49
  105.3 8.4 %collective-permute-done.18.v3 = bf16[128,2048]{1,0:T(8,128)(2,1)S(1)} collective-permute-done((bf16[128,2048]{1,0:T(8,128)(2,1)S(1)}, bf16[128,2048]{1,0:T(8,128)(2,1)S(1)}, u32[]{:S(2)}, u32[]{:S(2)}) %collective-permute-start.18) | collective-permute-done | bytes 524320 | tf_op jit(solution)/shard_map/ppermute | solution.py:49
  114.7 3.5 %all-to-all-start.2 = ((bf16[16,64,128]{2,1,0:T(8,128)(2,1)}), bf16[16,64,128]{2,1,0:T(8,128)(2,1)S(1)}, u32[]{:S(2)}, u32[]{:S(2)}) async-start(bf16[16,64,128]{2,1,0:T(8,128)(2,1)} %maximum_select_fusion), calls=%async_computation.2 | async-start | bytes 524288 | tf_op jit(solution)/shard_map/all_to_all | solution.py:58
  118.2 2.4 %collective-permute-start.20 = (bf16[128,2048]{1,0:T(8,128)(2,1)S(1)}, bf16[128,2048]{1,0:T(8,128)(2,1)S(1)}, u32[]{:S(2)}, u32[]{:S(2)}) collective-permute-start(bf16[128,2048]{1,0:T(8,128)(2,1)S(1)} %collective-permute-done.19.k1), channel_id=1, source_target_pairs={{0,96},{32,0},{64,32},{96,64},{1,97},{33,1},{65,33},{97,65},{2,98}... | collective-permute-start | bytes 1572872 | tf_op jit(solution)/shard_map/ppermute | solution.py:49
  120.6 5.4 %collective-permute-done.23.v1 = bf16[128,2048]{1,0:T(8,128)(2,1)} collective-permute-done((bf16[128,2048]{1,0:T(8,128)(2,1)S(1)}, bf16[128,2048]{1,0:T(8,128)(2,1)}, u32[]{:S(2)}, u32[]{:S(2)}) %collective-permute-start.23) | collective-permute-done | bytes 524320 | tf_op jit(solution)/shard_map/ppermute | solution.py:49
  126.0 2.9 %place_near.1 = (bf16[512,2048]{1,0:T(8,128)(2,1)}, bf16[512,2048]{1,0:T(8,128)(2,1)}) custom-call(bf16[128,2048]{1,0:T(8,128)(2,1)S(1)} %bitcast.20, bf16[128,2048]{1,0:T(8,128)(2,1)S(1)} %collective-permute-done.19.k1, bf16[128,2048]{1,0:T(8,128)(2,1)} %collective-permute-done.22.k3, bf16[128,2048]{1,0:T(8,128)(2,1)S(1)} %bitcast.23, ...), custom_call_target="tpu_custom_call" | custom-call | tf_op jit(solution)/shard_map/place_near/pallas_call | solution.py:379
  129.7 2.9 %collective-permute-done.20.k2 = bf16[128,2048]{1,0:T(8,128)(2,1)S(1)} collective-permute-done((bf16[128,2048]{1,0:T(8,128)(2,1)S(1)}, bf16[128,2048]{1,0:T(8,128)(2,1)S(1)}, u32[]{:S(2)}, u32[]{:S(2)}) %collective-permute-start.20) | collective-permute-done | bytes 524320 | tf_op jit(solution)/shard_map/ppermute | solution.py:49
  132.6 2.4 %place_far.1 = (bf16[512,2048]{1,0:T(8,128)(2,1)}, bf16[512,2048]{1,0:T(8,128)(2,1)}) custom-call(bf16[128,2048]{1,0:T(8,128)(2,1)S(1)} %collective-permute-done.20.k2, bf16[128,2048]{1,0:T(8,128)(2,1)S(1)} %collective-permute-done.21.v2, bf16[512,2048]{1,0:T(8,128)(2,1)} %get-tuple-element.51.ink, ...), custom_call_target="tpu_custom_call", output_to_operand_aliasing={{0}: (2, {}), {1}: (3, {})} | custom-call | tf_op jit(solution)/shard_map/place_far/pallas_call | solution.py:393
  (54 shorter events, 22.4 us)
Async XLA Ops:
  0.6 9.1 %collective-permute-start.1 = (s32[16,16]{1,0:T(8,128)}, s32[16,16]{1,0:T(8,128)S(1)}, u32[]{:S(2)}, u32[]{:S(2)}) collective-permute-start(s32[16,16]{1,0:T(8,128)} %l0.1), channel_id=1, source_target_pairs={{0,64},{32,96},{64,0},{96,32},{1,65},{33,97},{65,1},{97,33},{2,66}... | collective-permute-start | bytes 3080 | tf_op jit(solution)/shard_map/ppermute | solution.py:49
  4.7 5.0 %collective-permute-start = (s32[16,16]{1,0:T(8,128)}, s32[16,16]{1,0:T(8,128)S(1)}, u32[]{:S(2)}, u32[]{:S(2)}) collective-permute-start(s32[16,16]{1,0:T(8,128)} %l0.1), channel_id=1, source_target_pairs={{0,96},{32,0},{64,32},{96,64},{1,97},{33,1},{65,33},{97,65},{2,98}... | collective-permute-start | bytes 3080 | tf_op jit(solution)/shard_map/ppermute | solution.py:49
  5.4 5.1 %collective-permute-start.2 = (s32[16,16]{1,0:T(8,128)}, s32[16,16]{1,0:T(8,128)S(1)}, u32[]{:S(2)}, u32[]{:S(2)}) collective-permute-start(s32[16,16]{1,0:T(8,128)} %l0.1), channel_id=1, source_target_pairs={{0,32},{32,64},{64,96},{96,0},{1,33},{33,65},{65,97},{97,1},{2,34}... | collective-permute-start | bytes 3080 | tf_op jit(solution)/shard_map/ppermute | solution.py:49
  10.5 22.7 %all-to-all-start = ((bf16[16,256,128]{2,1,0:T(8,128)(2,1)}), bf16[16,256,128]{2,1,0:T(8,128)(2,1)S(1)}, u32[]{:S(2)}, u32[]{:S(2)}) async-start(bf16[16,256,128]{2,1,0:T(8,128)(2,1)} %get-tuple-element.30), calls=%async_computation | async-start | bytes 2097152 | tf_op jit(solution)/shard_map/all_to_all | solution.py:58
  17.5 10.3 %collective-permute-start.6 = (bf16[8,128,128]{2,1,0:T(8,128)(2,1)S(1)}, bf16[8,128,128]{2,1,0:T(8,128)(2,1)S(1)}, u32[]{:S(2)}, u32[]{:S(2)}) collective-permute-start(bf16[8,128,128]{2,1,0:T(8,128)(2,1)S(1)} %copy-done), channel_id=1, source_target_pairs={{0,96},{32,0},{64,32},{96,64},{1,97},{33,1},{65,33},{97,65},{2,98}... | collective-permute-start | bytes 786440 | tf_op jit(solution)/shard_map/ppermute | solution.py:49
  18.9 10.5 %collective-permute-start.3 = (bf16[8,128,128]{2,1,0:T(8,128)(2,1)S(1)}, bf16[8,128,128]{2,1,0:T(8,128)(2,1)S(1)}, u32[]{:S(2)}, u32[]{:S(2)}) collective-permute-start(bf16[8,128,128]{2,1,0:T(8,128)(2,1)S(1)} %copy-done), channel_id=1, source_target_pairs={{0,32},{32,64},{64,96},{96,0},{1,33},{33,65},{65,97},{97,1},{2,34}... | collective-permute-start | bytes 786440 | tf_op jit(solution)/shard_map/ppermute | solution.py:49
  19.6 12.8 %collective-permute-start.5 = (bf16[8,128,128]{2,1,0:T(8,128)(2,1)S(1)}, bf16[8,128,128]{2,1,0:T(8,128)(2,1)S(1)}, u32[]{:S(2)}, u32[]{:S(2)}) collective-permute-start(bf16[8,128,128]{2,1,0:T(8,128)(2,1)S(1)} %copy-done.1), channel_id=1, source_target_pairs={{0,32},{32,64},{64,96},{96,0},{1,33},{33,65},{65,97},{97,1},{2,34}... | collective-permute-start | bytes 786440 | tf_op jit(solution)/shard_map/ppermute | solution.py:49
  20.0 12.4 %collective-permute-start.4 = (bf16[8,128,128]{2,1,0:T(8,128)(2,1)S(1)}, bf16[8,128,128]{2,1,0:T(8,128)(2,1)S(1)}, u32[]{:S(2)}, u32[]{:S(2)}) collective-permute-start(bf16[8,128,128]{2,1,0:T(8,128)(2,1)S(1)} %copy-done.1), channel_id=1, source_target_pairs={{0,96},{32,0},{64,32},{96,64},{1,97},{33,1},{65,33},{97,65},{2,98}... | collective-permute-start | bytes 786440 | tf_op jit(solution)/shard_map/ppermute | solution.py:49
  33.2 10.8 %collective-permute-start.8 = (bf16[8,128,128]{2,1,0:T(8,128)(2,1)S(1)}, bf16[8,128,128]{2,1,0:T(8,128)(2,1)S(1)}, u32[]{:S(2)}, u32[]{:S(2)}) collective-permute-start(bf16[8,128,128]{2,1,0:T(8,128)(2,1)S(1)} %collective-permute-done.3.refs_2_.q3), channel_id=1, source_target_pairs={{0,32},{32,64},{64,96},{96,0},{1,33},{33,65},{65,97},{97,1},{2,34}... | collective-permute-start | bytes 786440 | tf_op jit(solution)/shard_map/ppermute | solution.py:49
  34.3 9.7 %collective-permute-start.9 = (bf16[8,128,128]{2,1,0:T(8,128)(2,1)S(1)}, bf16[8,128,128]{2,1,0:T(8,128)(2,1)S(1)}, u32[]{:S(2)}, u32[]{:S(2)}) collective-permute-start(bf16[8,128,128]{2,1,0:T(8,128)(2,1)S(1)} %collective-permute-done.4.refs_4_.g1), channel_id=1, source_target_pairs={{0,96},{32,0},{64,32},{96,64},{1,97},{33,1},{65,33},{97,65},{2,98}... | collective-permute-start | bytes 786440 | tf_op jit(solution)/shard_map/ppermute | solution.py:49
  46.9 4.6 %collective-permute-start.12 = (f32[3,32,128]{2,1,0:T(8,128)S(1)}, f32[3,32,128]{2,1,0:T(8,128)S(1)}, u32[]{:S(2)}, u32[]{:S(2)}) collective-permute-start(f32[3,32,128]{2,1,0:T(8,128)S(1)} %forward.3.s0), channel_id=1, source_target_pairs={{0,96},{32,0},{64,32},{96,64},{1,97},{33,1},{65,33},{97,65},{2,98}... | collective-permute-start | bytes 147464 | tf_op jit(solution)/shard_map/ppermute | solution.py:49
  49.6 5.6 %collective-permute-start.11 = (f32[3,32,128]{2,1,0:T(8,128)S(1)}, f32[3,32,128]{2,1,0:T(8,128)S(1)}, u32[]{:S(2)}, u32[]{:S(2)}) collective-permute-start(f32[3,32,128]{2,1,0:T(8,128)S(1)} %forward.3.s0), channel_id=1, source_target_pairs={{0,64},{32,96},{64,0},{96,32},{1,65},{33,97},{65,1},{97,33},{2,66}... | collective-permute-start | bytes 147464 | tf_op jit(solution)/shard_map/ppermute | solution.py:49
  50.5 5.3 %collective-permute-start.10 = (f32[3,32,128]{2,1,0:T(8,128)S(1)}, f32[3,32,128]{2,1,0:T(8,128)S(1)}, u32[]{:S(2)}, u32[]{:S(2)}) collective-permute-start(f32[3,32,128]{2,1,0:T(8,128)S(1)} %forward.3.s0), channel_id=1, source_target_pairs={{0,32},{32,64},{64,96},{96,0},{1,33},{33,65},{65,97},{97,1},{2,34}... | collective-permute-start | bytes 147464 | tf_op jit(solution)/shard_map/ppermute | solution.py:49
  73.4 23.8 %all-to-all-start.1 = ((bf16[16,256,128]{2,1,0:T(8,128)(2,1)}), bf16[16,256,128]{2,1,0:T(8,128)(2,1)S(1)}, u32[]{:S(2)}, u32[]{:S(2)}) async-start(bf16[16,256,128]{2,1,0:T(8,128)(2,1)} %add_convert_fusion), calls=%async_computation.1 | async-start | bytes 2097152 | tf_op jit(solution)/shard_map/all_to_all | solution.py:58
  79.1 21.8 %collective-permute-start.13 = (bf16[8,128,128]{2,1,0:T(8,128)(2,1)}, bf16[8,128,128]{2,1,0:T(8,128)(2,1)S(1)}, u32[]{:S(2)}, u32[]{:S(2)}) collective-permute-start(bf16[8,128,128]{2,1,0:T(8,128)(2,1)} %get-tuple-element.43), channel_id=1, source_target_pairs={{0,32},{32,64},{64,96},{96,0},{1,33},{33,65},{65,97},{97,1},{2,34}... | collective-permute-start | bytes 786440 | tf_op jit(solution)/shard_map/ppermute | solution.py:49
  81.3 19.6 %collective-permute-start.14 = (bf16[8,128,128]{2,1,0:T(8,128)(2,1)}, bf16[8,128,128]{2,1,0:T(8,128)(2,1)S(1)}, u32[]{:S(2)}, u32[]{:S(2)}) collective-permute-start(bf16[8,128,128]{2,1,0:T(8,128)(2,1)} %get-tuple-element.44), channel_id=1, source_target_pairs={{0,96},{32,0},{64,32},{96,64},{1,97},{33,1},{65,33},{97,65},{2,98}... | collective-permute-start | bytes 786440 | tf_op jit(solution)/shard_map/ppermute | solution.py:49
  82.4 18.5 %collective-permute-start.15 = (bf16[8,128,128]{2,1,0:T(8,128)(2,1)}, bf16[8,128,128]{2,1,0:T(8,128)(2,1)S(1)}, u32[]{:S(2)}, u32[]{:S(2)}) collective-permute-start(bf16[8,128,128]{2,1,0:T(8,128)(2,1)} %get-tuple-element.45), channel_id=1, source_target_pairs={{0,64},{32,96},{64,0},{96,32},{1,65},{33,97},{65,1},{97,33},{2,66}... | collective-permute-start | bytes 786440 | tf_op jit(solution)/shard_map/ppermute | solution.py:49
  97.6 16.1 %collective-permute-start.18 = (bf16[128,2048]{1,0:T(8,128)(2,1)S(1)}, bf16[128,2048]{1,0:T(8,128)(2,1)S(1)}, u32[]{:S(2)}, u32[]{:S(2)}) collective-permute-start(bf16[128,2048]{1,0:T(8,128)(2,1)S(1)} %bitcast.21), channel_id=1, source_target_pairs={{0,32},{32,64},{64,96},{96,0},{1,33},{33,65},{65,97},{97,1},{2,34}... | collective-permute-start | bytes 1572872 | tf_op jit(solution)/shard_map/ppermute | solution.py:49
  99.8 14.9 %collective-permute-start.19 = (bf16[128,2048]{1,0:T(8,128)(2,1)S(1)}, bf16[128,2048]{1,0:T(8,128)(2,1)S(1)}, u32[]{:S(2)}, u32[]{:S(2)}) collective-permute-start(bf16[128,2048]{1,0:T(8,128)(2,1)S(1)} %bitcast.18), channel_id=1, source_target_pairs={{0,96},{32,0},{64,32},{96,64},{1,97},{33,1},{65,33},{97,65},{2,98}... | collective-permute-start | bytes 1572872 | tf_op jit(solution)/shard_map/ppermute | solution.py:49
  101.1 24.9 %collective-permute-start.23 = (bf16[128,2048]{1,0:T(8,128)(2,1)S(1)}, bf16[128,2048]{1,0:T(8,128)(2,1)}, u32[]{:S(2)}, u32[]{:S(2)}) collective-permute-start(bf16[128,2048]{1,0:T(8,128)(2,1)S(1)} %bitcast.22), channel_id=1, source_target_pairs={{0,96},{32,0},{64,32},{96,64},{1,97},{33,1},{65,33},{97,65},{2,98}... | collective-permute-start | bytes 1572872 | tf_op jit(solution)/shard_map/ppermute | solution.py:49
  102.2 23.8 %collective-permute-start.22 = (bf16[128,2048]{1,0:T(8,128)(2,1)S(1)}, bf16[128,2048]{1,0:T(8,128)(2,1)}, u32[]{:S(2)}, u32[]{:S(2)}) collective-permute-start(bf16[128,2048]{1,0:T(8,128)(2,1)S(1)} %bitcast.19), channel_id=1, source_target_pairs={{0,32},{32,64},{64,96},{96,0},{1,33},{33,65},{65,97},{97,1},{2,34}... | collective-permute-start | bytes 1572872 | tf_op jit(solution)/shard_map/ppermute | solution.py:49
  114.7 14.3 %all-to-all-start.2 = ((bf16[16,64,128]{2,1,0:T(8,128)(2,1)}), bf16[16,64,128]{2,1,0:T(8,128)(2,1)S(1)}, u32[]{:S(2)}, u32[]{:S(2)}) async-start(bf16[16,64,128]{2,1,0:T(8,128)(2,1)} %maximum_select_fusion), calls=%async_computation.2 | async-start | bytes 524288 | tf_op jit(solution)/shard_map/all_to_all | solution.py:58
  118.2 14.4 %collective-permute-start.20 = (bf16[128,2048]{1,0:T(8,128)(2,1)S(1)}, bf16[128,2048]{1,0:T(8,128)(2,1)S(1)}, u32[]{:S(2)}, u32[]{:S(2)}) collective-permute-start(bf16[128,2048]{1,0:T(8,128)(2,1)S(1)} %collective-permute-done.19.k1), channel_id=1, source_target_pairs={{0,96},{32,0},{64,32},{96,64},{1,97},{33,1},{65,33},{97,65},{2,98}... | collective-permute-start | bytes 1572872 | tf_op jit(solution)/shard_map/ppermute | solution.py:49
  120.6 12.0 %collective-permute-start.21 = (bf16[128,2048]{1,0:T(8,128)(2,1)S(1)}, bf16[128,2048]{1,0:T(8,128)(2,1)S(1)}, u32[]{:S(2)}, u32[]{:S(2)}) collective-permute-start(bf16[128,2048]{1,0:T(8,128)(2,1)S(1)} %collective-permute-done.18.v3), channel_id=1, source_target_pairs={{0,32},{32,64},{64,96},{96,0},{1,33},{33,65},{65,97},{97,1},{2,34}... | collective-permute-start | bytes 1572872 | tf_op jit(solution)/shard_map/ppermute | solution.py:49
  (7 other events, 51.6 us)
where the time goes:
time: 136 us; the launch traced here: 135 us
  starting transfers between devices  46.8 us (34%)
  waiting for transfers between devices  46.8 us (34%)
  Pallas kernels  37.2 us (27%)
  other arithmetic  2.12 us (2%)
    ppermute x21, starting transfers between devices, over_z(): return lax.ppermute(array, 'dp', [(i, (i + shift) % NZ) for i in range(NZ)])  30.4 us
    ppermute x21, waiting for transfers between devices, over_z(): return lax.ppermute(array, 'dp', [(i, (i + shift) % NZ) for i in range(NZ)])  28.3 us
    all_to_all x3, starting transfers between devices, plane_exchange(): return lax.all_to_all(array, 'mem', 0, 0, axis_index_groups=groups)  16.3 us
    all_to_all x3, waiting for transfers between devices, plane_exchange(): return lax.all_to_all(array, 'mem', 0, 0, axis_index_groups=groups)  14.6 us
    pallas_call x1, Pallas kernels, backward(): pl.pallas_call(bwd_kernel, out_shape=tuple(outs), in_specs=[smem] + [vmem...  13.6 us
    pallas_call x2, Pallas kernels, forward(): pl.pallas_call(functools.partial(fwd_kernel, groups, start), out_shape=ja...  10.4 us
    pallas_call x1, Pallas kernels, make_list(): pl.pallas_call(list_kernel, out_shape=jax.ShapeDtypeStruct((COUNT + 8,),...  4.94 us
    ppermute x3, waiting for transfers between devices, swap_cores(): return lax.ppermute(array, 'mem', [(i, i ^ 1) for i in range(2 * NCHIP)])  3.98 us
  transfers between devices with their start and end apart: 27, of which 14 were waited for; matrix products, arithmetic and copies ran while one was open for 1% of the time, Pallas kernels for 14%

commit v1 on v0

--- a/solution.py
+++ b/solution.py
@@ -226,7 +226,7 @@
 def bwd_kernel(
     ents, s0, s1, s2, s3, q0, q1, q2, q3, g0, g1, g2, g3, kva, kvb,
     dq0, dq1, dq2, dq3, own, other,
-    qs, gs, kv, dq, dkv, away, dqs, lse, delta, sems, outsems,
+    qs, gs, kv, dq, dkv, dqs, lse, delta, sems, outsems,
 ):
     copies = fetch(range(NZ), (q0, q1, q2, q3), (g0, g1, g2, g3), (kva, kvb), qs, gs, kv, sems)
 
@@ -291,16 +291,13 @@
 
     lax.fori_loop(0, steps, body, 0)
     sends = []
-    for n, ref in ((1, other), (0, own)):
-        half = slice(n * NCHIP, (n + 1) * NCHIP)
-        away[half] = dkv[half].astype(BF)
-        sends.append(pltpu.make_async_copy(away.at[half], ref, outsems.at[n]))
-        sends[-1].start()
     for r, ref in enumerate((dq0, dq1, dq2, dq3)):
         part = slice(r * QPER, (r + 1) * QPER)
         dqs[part] = dq[part].astype(BF)
-        sends.append(pltpu.make_async_copy(dqs.at[part], ref, outsems.at[2 + r]))
+        sends.append(pltpu.make_async_copy(dqs.at[part], ref, outsems.at[r]))
         sends[-1].start()
+    other[...] = dkv[NCHIP:].astype(BF)
+    own[...] = dkv[:NCHIP].astype(BF)
     for send in sends:
         send.wait()
 
@@ -317,17 +314,16 @@
         bwd_kernel,
         out_shape=tuple(outs),
         in_specs=[smem] + [vmem] * 4 + [far] * 10,
-        out_specs=tuple([far] * 6),
+        out_specs=tuple([far] * 4 + [vmem] * 2),
         scratch_shapes=scratch_in()
         + [
             pltpu.VMEM((NQ,) + tile, F32),
             pltpu.VMEM((NB, 2 * BLK, DH), F32),
-            pltpu.VMEM((NB, 2 * BLK, DH), BF),
             pltpu.VMEM((NQ,) + tile, BF),
             pltpu.VMEM((2 * NQ, DH), F32),
             pltpu.VMEM((2 * NQ, DH), F32),
             pltpu.SemaphoreType.DMA((NCOPY,)),
-            pltpu.SemaphoreType.DMA((6,)),
+            pltpu.SemaphoreType.DMA((NZ,)),
         ],
         compiler_params=pltpu.CompilerParams(vmem_limit_bytes=24 * MB),
         name="backward",

time: 136 us -> 135 us (level)
  waiting for transfers between devices: 46.8 us -> 44.2 us
  starting transfers between devices: 46.8 us -> 49.3 us
    ppermute x21, starting transfers between devices: 30.4 us -> 32.7 us  [over_z(): return lax.ppermute(array, 'dp', [(i, (i + shift) % NZ) for i in range(NZ)])]
    ppermute x21, waiting for transfers between devices: 28.3 us -> 26.6 us  [over_z(): return lax.ppermute(array, 'dp', [(i, (i + shift) % NZ) for i in range(NZ)])]
  transfers between devices with their start and end apart: 27 -> 27, of which waited for: 14 -> 14; matrix products, arithmetic and copies ran while one was open for 1% -> 1% of each run, Pallas kernels for 14% -> 13%
where the time goes in v1:
time: 135 us; the launch traced here: 134 us
  starting transfers between devices  49.3 us (37%)
  waiting for transfers between devices  44.2 us (33%)
  Pallas kernels  36.3 us (27%)
  other arithmetic  2.12 us (2%)
    ppermute x21, starting transfers between devices, over_z(): return lax.ppermute(array, 'dp', [(i, (i + shift) % NZ) for i in range(NZ)])  32.7 us
    ppermute x21, waiting for transfers between devices, over_z(): return lax.ppermute(array, 'dp', [(i, (i + shift) % NZ) for i in range(NZ)])  26.6 us
    all_to_all x3, starting transfers between devices, plane_exchange(): return lax.all_to_all(array, 'mem', 0, 0, axis_index_groups=groups)  16.4 us
    all_to_all x3, waiting for transfers between devices, plane_exchange(): return lax.all_to_all(array, 'mem', 0, 0, axis_index_groups=groups)  13.7 us
    pallas_call x1, Pallas kernels, backward(): pl.pallas_call(bwd_kernel, out_shape=tuple(outs), in_specs=[smem] + [vmem...  13.2 us
    pallas_call x2, Pallas kernels, forward(): pl.pallas_call(functools.partial(fwd_kernel, groups, start), out_shape=ja...  9.95 us
    pallas_call x1, Pallas kernels, make_list(): pl.pallas_call(list_kernel, out_shape=jax.ShapeDtypeStruct((COUNT + 8,),...  4.94 us
    ppermute x3, waiting for transfers between devices, swap_cores(): return lax.ppermute(array, 'mem', [(i, i ^ 1) for i in range(2 * NCHIP)])  3.98 us
  transfers between devices with their start and end apart: 27, of which 14 were waited for; matrix products, arithmetic and copies ran while one was open for 1% of the time, Pallas kernels for 13%

profile of v1, /device:TPU:0, one launch (start us, length us, event | category | flops | bytes accessed | tf_op | source)
XLA Modules:
  0.0 134.0 jit_solution(3292291172804493246)
XLA Ops:
  0.6 4.0 %collective-permute-start.1 = (s32[16,16]{1,0:T(8,128)}, s32[16,16]{1,0:T(8,128)S(1)}, u32[]{:S(2)}, u32[]{:S(2)}) collective-permute-start(s32[16,16]{1,0:T(8,128)} %l0.1), channel_id=1, source_target_pairs={{0,64},{32,96},{64,0},{96,32},{1,65},{33,97},{65,1},{97,33},{2,66}... | collective-permute-start | bytes 3080 | tf_op jit(solution)/shard_map/ppermute | solution.py:49
  6.7 2.9 %prepare.1 = (bf16[8,128,128]{2,1,0:T(8,128)(2,1)}, bf16[8,128,128]{2,1,0:T(8,128)(2,1)}, bf16[16,256,128]{2,1,0:T(8,128)(2,1)}) custom-call(bf16[2048,2048]{1,0:T(8,128)(2,1)} %queries.1, bf16[2048,2048]{1,0:T(8,128)(2,1)} %grads.1, bf16[512,2048]{1,0:T(8,128)(2,1)} %keys.1, bf16[512,2048]{1,0:T(8,128)(2,1)} %values.1), custom_call_target="tpu_custom_call" | custom-call | tf_op jit(solution)/shard_map/prepare/pallas_call | solution.py:84
  10.5 7.0 %all-to-all-start = ((bf16[16,256,128]{2,1,0:T(8,128)(2,1)}), bf16[16,256,128]{2,1,0:T(8,128)(2,1)S(1)}, u32[]{:S(2)}, u32[]{:S(2)}) async-start(bf16[16,256,128]{2,1,0:T(8,128)(2,1)} %get-tuple-element.30), calls=%async_computation | async-start | bytes 2097152 | tf_op jit(solution)/shard_map/all_to_all | solution.py:58
  20.0 2.8 %collective-permute-start.4 = (bf16[8,128,128]{2,1,0:T(8,128)(2,1)S(1)}, bf16[8,128,128]{2,1,0:T(8,128)(2,1)S(1)}, u32[]{:S(2)}, u32[]{:S(2)}) collective-permute-start(bf16[8,128,128]{2,1,0:T(8,128)(2,1)S(1)} %copy-done.1), channel_id=1, source_target_pairs={{0,96},{32,0},{64,32},{96,64},{1,97},{33,1},{65,33},{97,65},{2,98}... | collective-permute-start | bytes 786440 | tf_op jit(solution)/shard_map/ppermute | solution.py:49
  22.9 4.9 %entry_list.1.ents = s32[544]{0:T(1024)S(1)} custom-call(s32[16,16]{1,0:T(8,128)S(1)} %copy-done.2, s32[16,16]{1,0:T(8,128)S(1)} %collective-permute-done.l1, s32[16,16]{1,0:T(8,128)S(1)} %collective-permute-done.1.l2, s32[16,16]{1,0:T(8,128)S(1)} %collective-permute-done.2.l3, s32[128]{0:T(128)S(1)} %copy-done.3), custom_call_target="tpu_custom_call" | custom-call | tf_op jit(solution)/shard_map/entry_list/pallas_call | solution.py:131
  29.4 3.0 %collective-permute-done.5.refs_5_.g3 = bf16[8,128,128]{2,1,0:T(8,128)(2,1)S(1)} collective-permute-done((bf16[8,128,128]{2,1,0:T(8,128)(2,1)S(1)}, bf16[8,128,128]{2,1,0:T(8,128)(2,1)S(1)}, u32[]{:S(2)}, u32[]{:S(2)}) %collective-permute-start.5) | collective-permute-done | bytes 262176 | tf_op jit(solution)/shard_map/ppermute | solution.py:49
  34.3 2.2 %collective-permute-start.9 = (bf16[8,128,128]{2,1,0:T(8,128)(2,1)S(1)}, bf16[8,128,128]{2,1,0:T(8,128)(2,1)S(1)}, u32[]{:S(2)}, u32[]{:S(2)}) collective-permute-start(bf16[8,128,128]{2,1,0:T(8,128)(2,1)S(1)} %collective-permute-done.4.refs_4_.g1), channel_id=1, source_target_pairs={{0,96},{32,0},{64,32},{96,64},{1,97},{33,1},{65,33},{97,65},{2,98}... | collective-permute-start | bytes 786440 | tf_op jit(solution)/shard_map/ppermute | solution.py:49
  36.4 7.0 %forward.2.before = f32[3,32,128]{2,1,0:T(8,128)S(1)} custom-call(s32[544]{0:T(1024)S(1)} %entry_list.1.ents, f32[3,32,128]{2,1,0:T(8,128)S(1)} %broadcast_in_dim.3.before, bf16[8,128,128]{2,1,0:T(8,128)(2,1)S(1)} %copy-done, bf16[8,128,128]{2,1,0:T(8,128)(2,1)S(1)} %collective-permute-done.6.refs_1_.q1, ...), custom_call_target="tpu_custom_call" | custom-call | tf_op jit(solution)/shard_map/forward/pallas_call | solution.py:214
  43.5 2.9 %forward.3.s0 = f32[3,32,128]{2,1,0:T(8,128)S(1)} custom-call(s32[544]{0:T(1024)S(1)} %entry_list.1.ents, f32[3,32,128]{2,1,0:T(8,128)S(1)} %forward.2.before, bf16[8,128,128]{2,1,0:T(8,128)(2,1)S(1)} %collective-permute-done.8.refs_0_.q2, bf16[8,128,128]{2,1,0:T(8,128)(2,1)S(1)} %collective-permute-done.9.refs_1_.g2, ...), custom_call_target="tpu_custom_call" | custom-call | tf_op jit(solution)/shard_map/forward/pallas_call | solution.py:214
  46.4 3.2 %collective-permute-start.12 = (f32[3,32,128]{2,1,0:T(8,128)S(1)}, f32[3,32,128]{2,1,0:T(8,128)S(1)}, u32[]{:S(2)}, u32[]{:S(2)}) collective-permute-start(f32[3,32,128]{2,1,0:T(8,128)S(1)} %forward.3.s0), channel_id=1, source_target_pairs={{0,96},{32,0},{64,32},{96,64},{1,97},{33,1},{65,33},{97,65},{2,98}... | collective-permute-start | bytes 147464 | tf_op jit(solution)/shard_map/ppermute | solution.py:49
  51.3 3.9 %collective-permute-done.11.s2 = f32[3,32,128]{2,1,0:T(8,128)S(1)} collective-permute-done((f32[3,32,128]{2,1,0:T(8,128)S(1)}, f32[3,32,128]{2,1,0:T(8,128)S(1)}, u32[]{:S(2)}, u32[]{:S(2)}) %collective-permute-start.11) | collective-permute-done | bytes 49184 | tf_op jit(solution)/shard_map/ppermute | solution.py:49
  55.7 13.2 %backward.1 = (bf16[8,128,128]{2,1,0:T(8,128)(2,1)S(1)}, bf16[8,128,128]{2,1,0:T(8,128)(2,1)}, bf16[8,128,128]{2,1,0:T(8,128)(2,1)}, bf16[8,128,128]{2,1,0:T(8,1...) custom-call(s32[544]{0:T(1024)S(1)} %entry_list.1.ents, f32[3,32,128]{2,1,0:T(8,128)S(1)} %forward.3.s0, ...), custom_call_target="tpu_custom_call" | custom-call | tf_op jit(solution)/shard_map/backward/pallas_call | solution.py:313
  69.0 2.6 %collective-permute-done.17 = bf16[16,256,128]{2,1,0:T(8,128)(2,1)S(1)} collective-permute-done((bf16[16,256,128]{2,1,0:T(8,128)(2,1)S(1)}, bf16[16,256,128]{2,1,0:T(8,128)(2,1)S(1)}, u32[]{:S(2)}, u32[]{:S(2)}) %collective-permute-start.17) | collective-permute-done | bytes 1048608 | tf_op jit(solution)/shard_map/ppermute | solution.py:53
  72.9 5.8 %all-to-all-start.1 = ((bf16[16,256,128]{2,1,0:T(8,128)(2,1)}), bf16[16,256,128]{2,1,0:T(8,128)(2,1)S(1)}, u32[]{:S(2)}, u32[]{:S(2)}) async-start(bf16[16,256,128]{2,1,0:T(8,128)(2,1)} %add_convert_fusion), calls=%async_computation.1 | async-start | bytes 2097152 | tf_op jit(solution)/shard_map/all_to_all | solution.py:58
  79.6 2.5 %collective-permute-start.14 = (bf16[8,128,128]{2,1,0:T(8,128)(2,1)}, bf16[8,128,128]{2,1,0:T(8,128)(2,1)S(1)}, u32[]{:S(2)}, u32[]{:S(2)}) collective-permute-start(bf16[8,128,128]{2,1,0:T(8,128)(2,1)} %get-tuple-element.44), channel_id=1, source_target_pairs={{0,96},{32,0},{64,32},{96,64},{1,97},{33,1},{65,33},{97,65},{2,98}... | collective-permute-start | bytes 786440 | tf_op jit(solution)/shard_map/ppermute | solution.py:49
  84.0 12.9 %all-to-all-done.1 = bf16[16,256,128]{2,1,0:T(8,128)(2,1)S(1)} async-done(((bf16[16,256,128]{2,1,0:T(8,128)(2,1)}), bf16[16,256,128]{2,1,0:T(8,128)(2,1)S(1)}, u32[]{:S(2)}, u32[]{:S(2)}) %all-to-all-start.1) | async-done | bytes 1048608 | tf_op jit(solution)/shard_map/all_to_all | solution.py:58
  98.1 2.5 %collective-permute-start.19 = (bf16[128,2048]{1,0:T(8,128)(2,1)S(1)}, bf16[128,2048]{1,0:T(8,128)(2,1)S(1)}, u32[]{:S(2)}, u32[]{:S(2)}) collective-permute-start(bf16[128,2048]{1,0:T(8,128)(2,1)S(1)} %bitcast.18), channel_id=1, source_target_pairs={{0,96},{32,0},{64,32},{96,64},{1,97},{33,1},{65,33},{97,65},{2,98}... | collective-permute-start | bytes 1572872 | tf_op jit(solution)/shard_map/ppermute | solution.py:49
  105.0 8.4 %collective-permute-done.18.v3 = bf16[128,2048]{1,0:T(8,128)(2,1)S(1)} collective-permute-done((bf16[128,2048]{1,0:T(8,128)(2,1)S(1)}, bf16[128,2048]{1,0:T(8,128)(2,1)S(1)}, u32[]{:S(2)}, u32[]{:S(2)}) %collective-permute-start.18) | collective-permute-done | bytes 524320 | tf_op jit(solution)/shard_map/ppermute | solution.py:49
  113.4 3.5 %all-to-all-start.2 = ((bf16[16,64,128]{2,1,0:T(8,128)(2,1)}), bf16[16,64,128]{2,1,0:T(8,128)(2,1)S(1)}, u32[]{:S(2)}, u32[]{:S(2)}) async-start(bf16[16,64,128]{2,1,0:T(8,128)(2,1)} %maximum_select_fusion), calls=%async_computation.2 | async-start | bytes 524288 | tf_op jit(solution)/shard_map/all_to_all | solution.py:58
  116.9 3.3 %collective-permute-start.20 = (bf16[128,2048]{1,0:T(8,128)(2,1)S(1)}, bf16[128,2048]{1,0:T(8,128)(2,1)S(1)}, u32[]{:S(2)}, u32[]{:S(2)}) collective-permute-start(bf16[128,2048]{1,0:T(8,128)(2,1)S(1)} %collective-permute-done.19.k1), channel_id=1, source_target_pairs={{0,96},{32,0},{64,32},{96,64},{1,97},{33,1},{65,33},{97,65},{2,98}... | collective-permute-start | bytes 1572872 | tf_op jit(solution)/shard_map/ppermute | solution.py:49
  120.2 4.3 %collective-permute-done.23.v1 = bf16[128,2048]{1,0:T(8,128)(2,1)} collective-permute-done((bf16[128,2048]{1,0:T(8,128)(2,1)S(1)}, bf16[128,2048]{1,0:T(8,128)(2,1)}, u32[]{:S(2)}, u32[]{:S(2)}) %collective-permute-start.23) | collective-permute-done | bytes 524320 | tf_op jit(solution)/shard_map/ppermute | solution.py:49
  124.6 2.9 %place_near.1 = (bf16[512,2048]{1,0:T(8,128)(2,1)}, bf16[512,2048]{1,0:T(8,128)(2,1)}) custom-call(bf16[128,2048]{1,0:T(8,128)(2,1)S(1)} %bitcast.20, bf16[128,2048]{1,0:T(8,128)(2,1)S(1)} %collective-permute-done.19.k1, bf16[128,2048]{1,0:T(8,128)(2,1)} %collective-permute-done.22.k3, bf16[128,2048]{1,0:T(8,128)(2,1)S(1)} %bitcast.23, ...), custom_call_target="tpu_custom_call" | custom-call | tf_op jit(solution)/shard_map/place_near/pallas_call | solution.py:375
  128.3 3.2 %collective-permute-done.20.k2 = bf16[128,2048]{1,0:T(8,128)(2,1)S(1)} collective-permute-done((bf16[128,2048]{1,0:T(8,128)(2,1)S(1)}, bf16[128,2048]{1,0:T(8,128)(2,1)S(1)}, u32[]{:S(2)}, u32[]{:S(2)}) %collective-permute-start.20) | collective-permute-done | bytes 524320 | tf_op jit(solution)/shard_map/ppermute | solution.py:49
  131.6 2.4 %place_far.1 = (bf16[512,2048]{1,0:T(8,128)(2,1)}, bf16[512,2048]{1,0:T(8,128)(2,1)}) custom-call(bf16[128,2048]{1,0:T(8,128)(2,1)S(1)} %collective-permute-done.20.k2, bf16[128,2048]{1,0:T(8,128)(2,1)S(1)} %collective-permute-done.21.v2, bf16[512,2048]{1,0:T(8,128)(2,1)} %get-tuple-element.51.ink, ...), custom_call_target="tpu_custom_call", output_to_operand_aliasing={{0}: (2, {}), {1}: (3, {})} | custom-call | tf_op jit(solution)/shard_map/place_far/pallas_call | solution.py:389
  (54 shorter events, 21.6 us)
Async XLA Ops:
  0.6 9.1 %collective-permute-start.1 = (s32[16,16]{1,0:T(8,128)}, s32[16,16]{1,0:T(8,128)S(1)}, u32[]{:S(2)}, u32[]{:S(2)}) collective-permute-start(s32[16,16]{1,0:T(8,128)} %l0.1), channel_id=1, source_target_pairs={{0,64},{32,96},{64,0},{96,32},{1,65},{33,97},{65,1},{97,33},{2,66}... | collective-permute-start | bytes 3080 | tf_op jit(solution)/shard_map/ppermute | solution.py:49
  4.7 5.0 %collective-permute-start = (s32[16,16]{1,0:T(8,128)}, s32[16,16]{1,0:T(8,128)S(1)}, u32[]{:S(2)}, u32[]{:S(2)}) collective-permute-start(s32[16,16]{1,0:T(8,128)} %l0.1), channel_id=1, source_target_pairs={{0,96},{32,0},{64,32},{96,64},{1,97},{33,1},{65,33},{97,65},{2,98}... | collective-permute-start | bytes 3080 | tf_op jit(solution)/shard_map/ppermute | solution.py:49
  5.4 5.1 %collective-permute-start.2 = (s32[16,16]{1,0:T(8,128)}, s32[16,16]{1,0:T(8,128)S(1)}, u32[]{:S(2)}, u32[]{:S(2)}) collective-permute-start(s32[16,16]{1,0:T(8,128)} %l0.1), channel_id=1, source_target_pairs={{0,32},{32,64},{64,96},{96,0},{1,33},{33,65},{65,97},{97,1},{2,34}... | collective-permute-start | bytes 3080 | tf_op jit(solution)/shard_map/ppermute | solution.py:49
  10.5 22.7 %all-to-all-start = ((bf16[16,256,128]{2,1,0:T(8,128)(2,1)}), bf16[16,256,128]{2,1,0:T(8,128)(2,1)S(1)}, u32[]{:S(2)}, u32[]{:S(2)}) async-start(bf16[16,256,128]{2,1,0:T(8,128)(2,1)} %get-tuple-element.30), calls=%async_computation | async-start | bytes 2097152 | tf_op jit(solution)/shard_map/all_to_all | solution.py:58
  17.5 10.3 %collective-permute-start.6 = (bf16[8,128,128]{2,1,0:T(8,128)(2,1)S(1)}, bf16[8,128,128]{2,1,0:T(8,128)(2,1)S(1)}, u32[]{:S(2)}, u32[]{:S(2)}) collective-permute-start(bf16[8,128,128]{2,1,0:T(8,128)(2,1)S(1)} %copy-done), channel_id=1, source_target_pairs={{0,96},{32,0},{64,32},{96,64},{1,97},{33,1},{65,33},{97,65},{2,98}... | collective-permute-start | bytes 786440 | tf_op jit(solution)/shard_map/ppermute | solution.py:49
  18.9 10.5 %collective-permute-start.3 = (bf16[8,128,128]{2,1,0:T(8,128)(2,1)S(1)}, bf16[8,128,128]{2,1,0:T(8,128)(2,1)S(1)}, u32[]{:S(2)}, u32[]{:S(2)}) collective-permute-start(bf16[8,128,128]{2,1,0:T(8,128)(2,1)S(1)} %copy-done), channel_id=1, source_target_pairs={{0,32},{32,64},{64,96},{96,0},{1,33},{33,65},{65,97},{97,1},{2,34}... | collective-permute-start | bytes 786440 | tf_op jit(solution)/shard_map/ppermute | solution.py:49
  19.6 12.8 %collective-permute-start.5 = (bf16[8,128,128]{2,1,0:T(8,128)(2,1)S(1)}, bf16[8,128,128]{2,1,0:T(8,128)(2,1)S(1)}, u32[]{:S(2)}, u32[]{:S(2)}) collective-permute-start(bf16[8,128,128]{2,1,0:T(8,128)(2,1)S(1)} %copy-done.1), channel_id=1, source_target_pairs={{0,32},{32,64},{64,96},{96,0},{1,33},{33,65},{65,97},{97,1},{2,34}... | collective-permute-start | bytes 786440 | tf_op jit(solution)/shard_map/ppermute | solution.py:49
  20.0 12.4 %collective-permute-start.4 = (bf16[8,128,128]{2,1,0:T(8,128)(2,1)S(1)}, bf16[8,128,128]{2,1,0:T(8,128)(2,1)S(1)}, u32[]{:S(2)}, u32[]{:S(2)}) collective-permute-start(bf16[8,128,128]{2,1,0:T(8,128)(2,1)S(1)} %copy-done.1), channel_id=1, source_target_pairs={{0,96},{32,0},{64,32},{96,64},{1,97},{33,1},{65,33},{97,65},{2,98}... | collective-permute-start | bytes 786440 | tf_op jit(solution)/shard_map/ppermute | solution.py:49
  33.2 10.3 %collective-permute-start.8 = (bf16[8,128,128]{2,1,0:T(8,128)(2,1)S(1)}, bf16[8,128,128]{2,1,0:T(8,128)(2,1)S(1)}, u32[]{:S(2)}, u32[]{:S(2)}) collective-permute-start(bf16[8,128,128]{2,1,0:T(8,128)(2,1)S(1)} %collective-permute-done.3.refs_2_.q3), channel_id=1, source_target_pairs={{0,32},{32,64},{64,96},{96,0},{1,33},{33,65},{65,97},{97,1},{2,34}... | collective-permute-start | bytes 786440 | tf_op jit(solution)/shard_map/ppermute | solution.py:49
  34.3 9.2 %collective-permute-start.9 = (bf16[8,128,128]{2,1,0:T(8,128)(2,1)S(1)}, bf16[8,128,128]{2,1,0:T(8,128)(2,1)S(1)}, u32[]{:S(2)}, u32[]{:S(2)}) collective-permute-start(bf16[8,128,128]{2,1,0:T(8,128)(2,1)S(1)} %collective-permute-done.4.refs_4_.g1), channel_id=1, source_target_pairs={{0,96},{32,0},{64,32},{96,64},{1,97},{33,1},{65,33},{97,65},{2,98}... | collective-permute-start | bytes 786440 | tf_op jit(solution)/shard_map/ppermute | solution.py:49
  46.4 4.9 %collective-permute-start.12 = (f32[3,32,128]{2,1,0:T(8,128)S(1)}, f32[3,32,128]{2,1,0:T(8,128)S(1)}, u32[]{:S(2)}, u32[]{:S(2)}) collective-permute-start(f32[3,32,128]{2,1,0:T(8,128)S(1)} %forward.3.s0), channel_id=1, source_target_pairs={{0,96},{32,0},{64,32},{96,64},{1,97},{33,1},{65,33},{97,65},{2,98}... | collective-permute-start | bytes 147464 | tf_op jit(solution)/shard_map/ppermute | solution.py:49
  49.6 5.6 %collective-permute-start.11 = (f32[3,32,128]{2,1,0:T(8,128)S(1)}, f32[3,32,128]{2,1,0:T(8,128)S(1)}, u32[]{:S(2)}, u32[]{:S(2)}) collective-permute-start(f32[3,32,128]{2,1,0:T(8,128)S(1)} %forward.3.s0), channel_id=1, source_target_pairs={{0,64},{32,96},{64,0},{96,32},{1,65},{33,97},{65,1},{97,33},{2,66}... | collective-permute-start | bytes 147464 | tf_op jit(solution)/shard_map/ppermute | solution.py:49
  50.0 5.7 %collective-permute-start.10 = (f32[3,32,128]{2,1,0:T(8,128)S(1)}, f32[3,32,128]{2,1,0:T(8,128)S(1)}, u32[]{:S(2)}, u32[]{:S(2)}) collective-permute-start(f32[3,32,128]{2,1,0:T(8,128)S(1)} %forward.3.s0), channel_id=1, source_target_pairs={{0,32},{32,64},{64,96},{96,0},{1,33},{33,65},{65,97},{97,1},{2,34}... | collective-permute-start | bytes 147464 | tf_op jit(solution)/shard_map/ppermute | solution.py:49
  72.9 24.0 %all-to-all-start.1 = ((bf16[16,256,128]{2,1,0:T(8,128)(2,1)}), bf16[16,256,128]{2,1,0:T(8,128)(2,1)S(1)}, u32[]{:S(2)}, u32[]{:S(2)}) async-start(bf16[16,256,128]{2,1,0:T(8,128)(2,1)} %add_convert_fusion), calls=%async_computation.1 | async-start | bytes 2097152 | tf_op jit(solution)/shard_map/all_to_all | solution.py:58
  78.8 21.8 %collective-permute-start.13 = (bf16[8,128,128]{2,1,0:T(8,128)(2,1)}, bf16[8,128,128]{2,1,0:T(8,128)(2,1)S(1)}, u32[]{:S(2)}, u32[]{:S(2)}) collective-permute-start(bf16[8,128,128]{2,1,0:T(8,128)(2,1)} %get-tuple-element.43), channel_id=1, source_target_pairs={{0,32},{32,64},{64,96},{96,0},{1,33},{33,65},{65,97},{97,1},{2,34}... | collective-permute-start | bytes 786440 | tf_op jit(solution)/shard_map/ppermute | solution.py:49
  79.6 21.0 %collective-permute-start.14 = (bf16[8,128,128]{2,1,0:T(8,128)(2,1)}, bf16[8,128,128]{2,1,0:T(8,128)(2,1)S(1)}, u32[]{:S(2)}, u32[]{:S(2)}) collective-permute-start(bf16[8,128,128]{2,1,0:T(8,128)(2,1)} %get-tuple-element.44), channel_id=1, source_target_pairs={{0,96},{32,0},{64,32},{96,64},{1,97},{33,1},{65,33},{97,65},{2,98}... | collective-permute-start | bytes 786440 | tf_op jit(solution)/shard_map/ppermute | solution.py:49
  82.1 18.5 %collective-permute-start.15 = (bf16[8,128,128]{2,1,0:T(8,128)(2,1)}, bf16[8,128,128]{2,1,0:T(8,128)(2,1)S(1)}, u32[]{:S(2)}, u32[]{:S(2)}) collective-permute-start(bf16[8,128,128]{2,1,0:T(8,128)(2,1)} %get-tuple-element.45), channel_id=1, source_target_pairs={{0,64},{32,96},{64,0},{96,32},{1,65},{33,97},{65,1},{97,33},{2,66}... | collective-permute-start | bytes 786440 | tf_op jit(solution)/shard_map/ppermute | solution.py:49
  97.2 16.1 %collective-permute-start.18 = (bf16[128,2048]{1,0:T(8,128)(2,1)S(1)}, bf16[128,2048]{1,0:T(8,128)(2,1)S(1)}, u32[]{:S(2)}, u32[]{:S(2)}) collective-permute-start(bf16[128,2048]{1,0:T(8,128)(2,1)S(1)} %bitcast.21), channel_id=1, source_target_pairs={{0,32},{32,64},{64,96},{96,0},{1,33},{33,65},{65,97},{97,1},{2,34}... | collective-permute-start | bytes 1572872 | tf_op jit(solution)/shard_map/ppermute | solution.py:49
  98.1 15.3 %collective-permute-start.19 = (bf16[128,2048]{1,0:T(8,128)(2,1)S(1)}, bf16[128,2048]{1,0:T(8,128)(2,1)S(1)}, u32[]{:S(2)}, u32[]{:S(2)}) collective-permute-start(bf16[128,2048]{1,0:T(8,128)(2,1)S(1)} %bitcast.18), channel_id=1, source_target_pairs={{0,96},{32,0},{64,32},{96,64},{1,97},{33,1},{65,33},{97,65},{2,98}... | collective-permute-start | bytes 1572872 | tf_op jit(solution)/shard_map/ppermute | solution.py:49
  100.7 23.9 %collective-permute-start.23 = (bf16[128,2048]{1,0:T(8,128)(2,1)S(1)}, bf16[128,2048]{1,0:T(8,128)(2,1)}, u32[]{:S(2)}, u32[]{:S(2)}) collective-permute-start(bf16[128,2048]{1,0:T(8,128)(2,1)S(1)} %bitcast.22), channel_id=1, source_target_pairs={{0,96},{32,0},{64,32},{96,64},{1,97},{33,1},{65,33},{97,65},{2,98}... | collective-permute-start | bytes 1572872 | tf_op jit(solution)/shard_map/ppermute | solution.py:49
  101.3 23.3 %collective-permute-start.22 = (bf16[128,2048]{1,0:T(8,128)(2,1)S(1)}, bf16[128,2048]{1,0:T(8,128)(2,1)}, u32[]{:S(2)}, u32[]{:S(2)}) collective-permute-start(bf16[128,2048]{1,0:T(8,128)(2,1)S(1)} %bitcast.19), channel_id=1, source_target_pairs={{0,32},{32,64},{64,96},{96,0},{1,33},{33,65},{65,97},{97,1},{2,34}... | collective-permute-start | bytes 1572872 | tf_op jit(solution)/shard_map/ppermute | solution.py:49
  113.4 14.1 %all-to-all-start.2 = ((bf16[16,64,128]{2,1,0:T(8,128)(2,1)}), bf16[16,64,128]{2,1,0:T(8,128)(2,1)S(1)}, u32[]{:S(2)}, u32[]{:S(2)}) async-start(bf16[16,64,128]{2,1,0:T(8,128)(2,1)} %maximum_select_fusion), calls=%async_computation.2 | async-start | bytes 524288 | tf_op jit(solution)/shard_map/all_to_all | solution.py:58
  116.9 14.5 %collective-permute-start.20 = (bf16[128,2048]{1,0:T(8,128)(2,1)S(1)}, bf16[128,2048]{1,0:T(8,128)(2,1)S(1)}, u32[]{:S(2)}, u32[]{:S(2)}) collective-permute-start(bf16[128,2048]{1,0:T(8,128)(2,1)S(1)} %collective-permute-done.19.k1), channel_id=1, source_target_pairs={{0,96},{32,0},{64,32},{96,64},{1,97},{33,1},{65,33},{97,65},{2,98}... | collective-permute-start | bytes 1572872 | tf_op jit(solution)/shard_map/ppermute | solution.py:49
  120.2 11.3 %collective-permute-start.21 = (bf16[128,2048]{1,0:T(8,128)(2,1)S(1)}, bf16[128,2048]{1,0:T(8,128)(2,1)S(1)}, u32[]{:S(2)}, u32[]{:S(2)}) collective-permute-start(bf16[128,2048]{1,0:T(8,128)(2,1)S(1)} %collective-permute-done.18.v3), channel_id=1, source_target_pairs={{0,32},{32,64},{64,96},{96,0},{1,33},{33,65},{65,97},{97,1},{2,34}... | collective-permute-start | bytes 1572872 | tf_op jit(solution)/shard_map/ppermute | solution.py:49
  (7 other events, 51.6 us)

commit v2 on v1

--- a/solution.py
+++ b/solution.py
@@ -22,7 +22,6 @@
 LATE_AT = len(EARLY) * QPER * TOPB + 8
 COUNT = LATE_AT + len(LATE) * QPER * TOPB + 16
 NCOPY = 2 * NZ + 2
-CHUNKS = 4
 UNROLL_F = 8
 UNROLL_B = 16
 SCALE = DH ** (-0.5)
@@ -279,14 +278,12 @@
             (x * (d - delta[pl.ds(p[2], 1), :]) * SCALE).astype(BF)
             for x, d, p in zip(probs, dprob, parts)
         ]
-        gv = [dot(x.astype(BF), b, NN) for x, b in zip(probs, grad)]
-        gk = [dot(x, b, NN) for x, b in zip(dscore, quer)]
-        gq = [dot(x, b, TN) for x, b in zip(dscore, keys)]
-        for p, a, b, c in zip(parts, gv, gk, gq):
+        probs = [x.astype(BF) for x in probs]
+        for p, x, d, key, que, gra in zip(parts, probs, dscore, keys, quer, grad):
             at = p[4] * NCHIP + p[5]
-            dkv[at, BLK:] += a
-            dkv[at, :BLK] += b
-            dq[p[0] * QPER + p[1]] += c
+            dkv[at, BLK:] += dot(x, gra, NN)
+            dkv[at, :BLK] += dot(d, que, NN)
+            dq[p[0] * QPER + p[1]] += dot(d, key, TN)
         return carry
 
     lax.fori_loop(0, steps, body, 0)
@@ -347,24 +344,8 @@
     place_parts(position()[0], parts, sems)
 
 
-def far_kernel(k2, v2, ink, inv, outk, outv, held, insems, outsems):
-    z = position()[0]
-    rows = BLK // CHUNKS
-    came, went = [], []
-    for n in range(CHUNKS):
-        for t, (ref, out) in enumerate(((k2, outk), (v2, outv))):
-            at = pl.ds(n * rows, rows)
-            to = pl.ds(pl.multiple_of(((z + 2) & 3) * BLK + n * rows, rows), rows)
-            s = 2 * n + t
-            came.append(pltpu.make_async_copy(ref.at[at], held.at[t, at], insems.at[s]))
-            went.append(pltpu.make_async_copy(held.at[t, at], out.at[to], outsems.at[s]))
-    for copy in came:
-        copy.start()
-    for first, second in zip(came, went):
-        first.wait()
-        second.start()
-    for copy in went:
-        copy.wait()
+def far_kernel(k2, v2, ink, inv, outk, outv, sems):
+    place_parts(position()[0], [(2, k2, outk), (2, v2, outv)], sems)
 
 
 def place_near(kparts, vparts):
@@ -389,13 +370,9 @@
     return pl.pallas_call(
         far_kernel,
         out_shape=(shape, shape),
-        in_specs=[far] * 4,
+        in_specs=[pl.BlockSpec(memory_space=pltpu.VMEM)] * 2 + [far] * 2,
         out_specs=(far, far),
-        scratch_shapes=[
-            pltpu.VMEM((2, BLK, H * DH), BF),
-            pltpu.SemaphoreType.DMA((2 * CHUNKS,)),
-            pltpu.SemaphoreType.DMA((2 * CHUNKS,)),
-        ],
+        scratch_shapes=[pltpu.SemaphoreType.DMA((2,))],
         input_output_aliases={2: 0, 3: 1},
         compiler_params=pltpu.CompilerParams(vmem_limit_bytes=8 * MB),
         name="place_far",

time: 135 us -> 134 us (level)
  Pallas kernels: 36.3 us -> 33.7 us
    ppermute x21, waiting for transfers between devices: 26.6 us -> 28.5 us  [over_z(): return lax.ppermute(array, 'dp', [(i, (i + shift) % NZ) for i in range(NZ)])]
    pallas_call x1, Pallas kernels: 2.42 us -> 0.98 us  [place_far(): pl.pallas_call(far_kernel, out_shape=(shape, shape), in_specs=[pl.BlockSp...]
  transfers between devices with their start and end apart: 27 -> 27, of which waited for: 14 -> 15; matrix products, arithmetic and copies ran while one was open for 1% -> 1% of each run, Pallas kernels for 13% -> 13%
where the time goes in v2:
time: 134 us; the launch traced here: 133 us
  starting transfers between devices  50.5 us (38%)
  waiting for transfers between devices  45 us (34%)
  Pallas kernels  33.7 us (25%)
  other arithmetic  2.12 us (2%)
    ppermute x21, starting transfers between devices, over_z(): return lax.ppermute(array, 'dp', [(i, (i + shift) % NZ) for i in range(NZ)])  33.7 us
    ppermute x21, waiting for transfers between devices, over_z(): return lax.ppermute(array, 'dp', [(i, (i + shift) % NZ) for i in range(NZ)])  28.5 us
    all_to_all x3, starting transfers between devices, plane_exchange(): return lax.all_to_all(array, 'mem', 0, 0, axis_index_groups=groups)  16.7 us
    all_to_all x3, waiting for transfers between devices, plane_exchange(): return lax.all_to_all(array, 'mem', 0, 0, axis_index_groups=groups)  12.5 us
    pallas_call x1, Pallas kernels, backward(): pl.pallas_call(bwd_kernel, out_shape=tuple(outs), in_specs=[smem] + [vmem...  12.5 us
    pallas_call x2, Pallas kernels, forward(): pl.pallas_call(functools.partial(fwd_kernel, groups, start), out_shape=ja...  9.44 us
    pallas_call x1, Pallas kernels, make_list(): pl.pallas_call(list_kernel, out_shape=jax.ShapeDtypeStruct((COUNT + 8,),...  4.94 us
    ppermute x3, waiting for transfers between devices, swap_cores(): return lax.ppermute(array, 'mem', [(i, i ^ 1) for i in range(2 * NCHIP)])  3.98 us
  transfers between devices with their start and end apart: 27, of which 15 were waited for; matrix products, arithmetic and copies ran while one was open for 1% of the time, Pallas kernels for 13%

profile of v2, /device:TPU:0, one launch (start us, length us, event | category | flops | bytes accessed | tf_op | source)
XLA Modules:
  0.0 133.4 jit_solution(17689724857466015800)
XLA Ops:
  0.6 4.0 %collective-permute-start.1 = (s32[16,16]{1,0:T(8,128)}, s32[16,16]{1,0:T(8,128)S(1)}, u32[]{:S(2)}, u32[]{:S(2)}) collective-permute-start(s32[16,16]{1,0:T(8,128)} %l0.1), channel_id=1, source_target_pairs={{0,64},{32,96},{64,0},{96,32},{1,65},{33,97},{65,1},{97,33},{2,66}... | collective-permute-start | bytes 3080 | tf_op jit(solution)/shard_map/ppermute | solution.py:48
  6.7 2.9 %prepare.1 = (bf16[8,128,128]{2,1,0:T(8,128)(2,1)}, bf16[8,128,128]{2,1,0:T(8,128)(2,1)}, bf16[16,256,128]{2,1,0:T(8,128)(2,1)}) custom-call(bf16[2048,2048]{1,0:T(8,128)(2,1)} %queries.1, bf16[2048,2048]{1,0:T(8,128)(2,1)} %grads.1, bf16[512,2048]{1,0:T(8,128)(2,1)} %keys.1, bf16[512,2048]{1,0:T(8,128)(2,1)} %values.1), custom_call_target="tpu_custom_call" | custom-call | tf_op jit(solution)/shard_map/prepare/pallas_call | solution.py:83
  10.5 7.0 %all-to-all-start = ((bf16[16,256,128]{2,1,0:T(8,128)(2,1)}), bf16[16,256,128]{2,1,0:T(8,128)(2,1)S(1)}, u32[]{:S(2)}, u32[]{:S(2)}) async-start(bf16[16,256,128]{2,1,0:T(8,128)(2,1)} %get-tuple-element.30), calls=%async_computation | async-start | bytes 2097152 | tf_op jit(solution)/shard_map/all_to_all | solution.py:57
  20.0 2.8 %collective-permute-start.4 = (bf16[8,128,128]{2,1,0:T(8,128)(2,1)S(1)}, bf16[8,128,128]{2,1,0:T(8,128)(2,1)S(1)}, u32[]{:S(2)}, u32[]{:S(2)}) collective-permute-start(bf16[8,128,128]{2,1,0:T(8,128)(2,1)S(1)} %copy-done.1), channel_id=1, source_target_pairs={{0,96},{32,0},{64,32},{96,64},{1,97},{33,1},{65,33},{97,65},{2,98}... | collective-permute-start | bytes 786440 | tf_op jit(solution)/shard_map/ppermute | solution.py:48
  22.9 4.9 %entry_list.1.ents = s32[544]{0:T(1024)S(1)} custom-call(s32[16,16]{1,0:T(8,128)S(1)} %copy-done.2, s32[16,16]{1,0:T(8,128)S(1)} %collective-permute-done.l1, s32[16,16]{1,0:T(8,128)S(1)} %collective-permute-done.1.l2, s32[16,16]{1,0:T(8,128)S(1)} %collective-permute-done.2.l3, s32[128]{0:T(128)S(1)} %copy-done.3), custom_call_target="tpu_custom_call" | custom-call | tf_op jit(solution)/shard_map/entry_list/pallas_call | solution.py:130
  29.4 3.0 %collective-permute-done.5.refs_5_.g3 = bf16[8,128,128]{2,1,0:T(8,128)(2,1)S(1)} collective-permute-done((bf16[8,128,128]{2,1,0:T(8,128)(2,1)S(1)}, bf16[8,128,128]{2,1,0:T(8,128)(2,1)S(1)}, u32[]{:S(2)}, u32[]{:S(2)}) %collective-permute-start.5) | collective-permute-done | bytes 262176 | tf_op jit(solution)/shard_map/ppermute | solution.py:48
  34.3 2.2 %collective-permute-start.9 = (bf16[8,128,128]{2,1,0:T(8,128)(2,1)S(1)}, bf16[8,128,128]{2,1,0:T(8,128)(2,1)S(1)}, u32[]{:S(2)}, u32[]{:S(2)}) collective-permute-start(bf16[8,128,128]{2,1,0:T(8,128)(2,1)S(1)} %collective-permute-done.4.refs_4_.g1), channel_id=1, source_target_pairs={{0,96},{32,0},{64,32},{96,64},{1,97},{33,1},{65,33},{97,65},{2,98}... | collective-permute-start | bytes 786440 | tf_op jit(solution)/shard_map/ppermute | solution.py:48
  36.4 6.5 %forward.2.before = f32[3,32,128]{2,1,0:T(8,128)S(1)} custom-call(s32[544]{0:T(1024)S(1)} %entry_list.1.ents, f32[3,32,128]{2,1,0:T(8,128)S(1)} %broadcast_in_dim.3.before, bf16[8,128,128]{2,1,0:T(8,128)(2,1)S(1)} %copy-done, bf16[8,128,128]{2,1,0:T(8,128)(2,1)S(1)} %collective-permute-done.6.refs_1_.q1, ...), custom_call_target="tpu_custom_call" | custom-call | tf_op jit(solution)/shard_map/forward/pallas_call | solution.py:213
  43.1 2.9 %forward.3.s0 = f32[3,32,128]{2,1,0:T(8,128)S(1)} custom-call(s32[544]{0:T(1024)S(1)} %entry_list.1.ents, f32[3,32,128]{2,1,0:T(8,128)S(1)} %forward.2.before, bf16[8,128,128]{2,1,0:T(8,128)(2,1)S(1)} %collective-permute-done.8.refs_0_.q2, bf16[8,128,128]{2,1,0:T(8,128)(2,1)S(1)} %collective-permute-done.9.refs_1_.g2, ...), custom_call_target="tpu_custom_call" | custom-call | tf_op jit(solution)/shard_map/forward/pallas_call | solution.py:213
  46.1 4.0 %collective-permute-start.12 = (f32[3,32,128]{2,1,0:T(8,128)S(1)}, f32[3,32,128]{2,1,0:T(8,128)S(1)}, u32[]{:S(2)}, u32[]{:S(2)}) collective-permute-start(f32[3,32,128]{2,1,0:T(8,128)S(1)} %forward.3.s0), channel_id=1, source_target_pairs={{0,96},{32,0},{64,32},{96,64},{1,97},{33,1},{65,33},{97,65},{2,98}... | collective-permute-start | bytes 147464 | tf_op jit(solution)/shard_map/ppermute | solution.py:48
  51.8 3.9 %collective-permute-done.11.s2 = f32[3,32,128]{2,1,0:T(8,128)S(1)} collective-permute-done((f32[3,32,128]{2,1,0:T(8,128)S(1)}, f32[3,32,128]{2,1,0:T(8,128)S(1)}, u32[]{:S(2)}, u32[]{:S(2)}) %collective-permute-start.11) | collective-permute-done | bytes 49184 | tf_op jit(solution)/shard_map/ppermute | solution.py:48
  55.9 12.5 %backward.1 = (bf16[8,128,128]{2,1,0:T(8,128)(2,1)S(1)}, bf16[8,128,128]{2,1,0:T(8,128)(2,1)}, bf16[8,128,128]{2,1,0:T(8,128)(2,1)}, bf16[8,128,128]{2,1,0:T(8,1...) custom-call(s32[544]{0:T(1024)S(1)} %entry_list.1.ents, f32[3,32,128]{2,1,0:T(8,128)S(1)} %forward.3.s0, ...), custom_call_target="tpu_custom_call" | custom-call | tf_op jit(solution)/shard_map/backward/pallas_call | solution.py:310
  68.5 2.6 %collective-permute-done.17 = bf16[16,256,128]{2,1,0:T(8,128)(2,1)S(1)} collective-permute-done((bf16[16,256,128]{2,1,0:T(8,128)(2,1)S(1)}, bf16[16,256,128]{2,1,0:T(8,128)(2,1)S(1)}, u32[]{:S(2)}, u32[]{:S(2)}) %collective-permute-start.17) | collective-permute-done | bytes 1048608 | tf_op jit(solution)/shard_map/ppermute | solution.py:52
  72.4 6.1 %all-to-all-start.1 = ((bf16[16,256,128]{2,1,0:T(8,128)(2,1)}), bf16[16,256,128]{2,1,0:T(8,128)(2,1)S(1)}, u32[]{:S(2)}, u32[]{:S(2)}) async-start(bf16[16,256,128]{2,1,0:T(8,128)(2,1)} %add_convert_fusion), calls=%async_computation.1 | async-start | bytes 2097152 | tf_op jit(solution)/shard_map/all_to_all | solution.py:57
  78.6 3.2 %collective-permute-start.14 = (bf16[8,128,128]{2,1,0:T(8,128)(2,1)}, bf16[8,128,128]{2,1,0:T(8,128)(2,1)S(1)}, u32[]{:S(2)}, u32[]{:S(2)}) collective-permute-start(bf16[8,128,128]{2,1,0:T(8,128)(2,1)} %get-tuple-element.44), channel_id=1, source_target_pairs={{0,96},{32,0},{64,32},{96,64},{1,97},{33,1},{65,33},{97,65},{2,98}... | collective-permute-start | bytes 786440 | tf_op jit(solution)/shard_map/ppermute | solution.py:48
  81.9 3.1 %collective-permute-start.15 = (bf16[8,128,128]{2,1,0:T(8,128)(2,1)}, bf16[8,128,128]{2,1,0:T(8,128)(2,1)S(1)}, u32[]{:S(2)}, u32[]{:S(2)}) collective-permute-start(bf16[8,128,128]{2,1,0:T(8,128)(2,1)} %get-tuple-element.45), channel_id=1, source_target_pairs={{0,64},{32,96},{64,0},{96,32},{1,65},{33,97},{65,1},{97,33},{2,66}... | collective-permute-start | bytes 786440 | tf_op jit(solution)/shard_map/ppermute | solution.py:48
  85.0 11.7 %all-to-all-done.1 = bf16[16,256,128]{2,1,0:T(8,128)(2,1)S(1)} async-done(((bf16[16,256,128]{2,1,0:T(8,128)(2,1)}), bf16[16,256,128]{2,1,0:T(8,128)(2,1)S(1)}, u32[]{:S(2)}, u32[]{:S(2)}) %all-to-all-start.1) | async-done | bytes 1048608 | tf_op jit(solution)/shard_map/all_to_all | solution.py:57
  97.1 3.2 %collective-permute-start.19 = (bf16[128,2048]{1,0:T(8,128)(2,1)S(1)}, bf16[128,2048]{1,0:T(8,128)(2,1)S(1)}, u32[]{:S(2)}, u32[]{:S(2)}) collective-permute-start(bf16[128,2048]{1,0:T(8,128)(2,1)S(1)} %bitcast.18), channel_id=1, source_target_pairs={{0,96},{32,0},{64,32},{96,64},{1,97},{33,1},{65,33},{97,65},{2,98}... | collective-permute-start | bytes 1572872 | tf_op jit(solution)/shard_map/ppermute | solution.py:48
  104.8 8.4 %collective-permute-done.18.v3 = bf16[128,2048]{1,0:T(8,128)(2,1)S(1)} collective-permute-done((bf16[128,2048]{1,0:T(8,128)(2,1)S(1)}, bf16[128,2048]{1,0:T(8,128)(2,1)S(1)}, u32[]{:S(2)}, u32[]{:S(2)}) %collective-permute-start.18) | collective-permute-done | bytes 524320 | tf_op jit(solution)/shard_map/ppermute | solution.py:48
  114.2 3.5 %all-to-all-start.2 = ((bf16[16,64,128]{2,1,0:T(8,128)(2,1)}), bf16[16,64,128]{2,1,0:T(8,128)(2,1)S(1)}, u32[]{:S(2)}, u32[]{:S(2)}) async-start(bf16[16,64,128]{2,1,0:T(8,128)(2,1)} %maximum_select_fusion), calls=%async_computation.2 | async-start | bytes 524288 | tf_op jit(solution)/shard_map/all_to_all | solution.py:57
  117.8 2.3 %collective-permute-start.20 = (bf16[128,2048]{1,0:T(8,128)(2,1)S(1)}, bf16[128,2048]{1,0:T(8,128)(2,1)S(1)}, u32[]{:S(2)}, u32[]{:S(2)}) collective-permute-start(bf16[128,2048]{1,0:T(8,128)(2,1)S(1)} %collective-permute-done.19.k1), channel_id=1, source_target_pairs={{0,96},{32,0},{64,32},{96,64},{1,97},{33,1},{65,33},{97,65},{2,98}... | collective-permute-start | bytes 1572872 | tf_op jit(solution)/shard_map/ppermute | solution.py:48
  120.0 5.5 %collective-permute-done.23.v1 = bf16[128,2048]{1,0:T(8,128)(2,1)} collective-permute-done((bf16[128,2048]{1,0:T(8,128)(2,1)S(1)}, bf16[128,2048]{1,0:T(8,128)(2,1)}, u32[]{:S(2)}, u32[]{:S(2)}) %collective-permute-start.23) | collective-permute-done | bytes 524320 | tf_op jit(solution)/shard_map/ppermute | solution.py:48
  125.6 2.9 %place_near.1 = (bf16[512,2048]{1,0:T(8,128)(2,1)}, bf16[512,2048]{1,0:T(8,128)(2,1)}) custom-call(bf16[128,2048]{1,0:T(8,128)(2,1)S(1)} %bitcast.20, bf16[128,2048]{1,0:T(8,128)(2,1)S(1)} %collective-permute-done.19.k1, bf16[128,2048]{1,0:T(8,128)(2,1)} %collective-permute-done.22.k3, bf16[128,2048]{1,0:T(8,128)(2,1)S(1)} %bitcast.23, ...), custom_call_target="tpu_custom_call" | custom-call | tf_op jit(solution)/shard_map/place_near/pallas_call | solution.py:356
  129.2 3.2 %collective-permute-done.20.k2 = bf16[128,2048]{1,0:T(8,128)(2,1)S(1)} collective-permute-done((bf16[128,2048]{1,0:T(8,128)(2,1)S(1)}, bf16[128,2048]{1,0:T(8,128)(2,1)S(1)}, u32[]{:S(2)}, u32[]{:S(2)}) %collective-permute-start.20) | collective-permute-done | bytes 524320 | tf_op jit(solution)/shard_map/ppermute | solution.py:48
  (54 shorter events, 19.8 us)
Async XLA Ops:
  0.6 9.1 %collective-permute-start.1 = (s32[16,16]{1,0:T(8,128)}, s32[16,16]{1,0:T(8,128)S(1)}, u32[]{:S(2)}, u32[]{:S(2)}) collective-permute-start(s32[16,16]{1,0:T(8,128)} %l0.1), channel_id=1, source_target_pairs={{0,64},{32,96},{64,0},{96,32},{1,65},{33,97},{65,1},{97,33},{2,66}... | collective-permute-start | bytes 3080 | tf_op jit(solution)/shard_map/ppermute | solution.py:48
  4.7 5.0 %collective-permute-start = (s32[16,16]{1,0:T(8,128)}, s32[16,16]{1,0:T(8,128)S(1)}, u32[]{:S(2)}, u32[]{:S(2)}) collective-permute-start(s32[16,16]{1,0:T(8,128)} %l0.1), channel_id=1, source_target_pairs={{0,96},{32,0},{64,32},{96,64},{1,97},{33,1},{65,33},{97,65},{2,98}... | collective-permute-start | bytes 3080 | tf_op jit(solution)/shard_map/ppermute | solution.py:48
  5.4 5.1 %collective-permute-start.2 = (s32[16,16]{1,0:T(8,128)}, s32[16,16]{1,0:T(8,128)S(1)}, u32[]{:S(2)}, u32[]{:S(2)}) collective-permute-start(s32[16,16]{1,0:T(8,128)} %l0.1), channel_id=1, source_target_pairs={{0,32},{32,64},{64,96},{96,0},{1,33},{33,65},{65,97},{97,1},{2,34}... | collective-permute-start | bytes 3080 | tf_op jit(solution)/shard_map/ppermute | solution.py:48
  10.5 22.7 %all-to-all-start = ((bf16[16,256,128]{2,1,0:T(8,128)(2,1)}), bf16[16,256,128]{2,1,0:T(8,128)(2,1)S(1)}, u32[]{:S(2)}, u32[]{:S(2)}) async-start(bf16[16,256,128]{2,1,0:T(8,128)(2,1)} %get-tuple-element.30), calls=%async_computation | async-start | bytes 2097152 | tf_op jit(solution)/shard_map/all_to_all | solution.py:57
  17.5 10.3 %collective-permute-start.6 = (bf16[8,128,128]{2,1,0:T(8,128)(2,1)S(1)}, bf16[8,128,128]{2,1,0:T(8,128)(2,1)S(1)}, u32[]{:S(2)}, u32[]{:S(2)}) collective-permute-start(bf16[8,128,128]{2,1,0:T(8,128)(2,1)S(1)} %copy-done), channel_id=1, source_target_pairs={{0,96},{32,0},{64,32},{96,64},{1,97},{33,1},{65,33},{97,65},{2,98}... | collective-permute-start | bytes 786440 | tf_op jit(solution)/shard_map/ppermute | solution.py:48
  18.9 10.5 %collective-permute-start.3 = (bf16[8,128,128]{2,1,0:T(8,128)(2,1)S(1)}, bf16[8,128,128]{2,1,0:T(8,128)(2,1)S(1)}, u32[]{:S(2)}, u32[]{:S(2)}) collective-permute-start(bf16[8,128,128]{2,1,0:T(8,128)(2,1)S(1)} %copy-done), channel_id=1, source_target_pairs={{0,32},{32,64},{64,96},{96,0},{1,33},{33,65},{65,97},{97,1},{2,34}... | collective-permute-start | bytes 786440 | tf_op jit(solution)/shard_map/ppermute | solution.py:48
  19.6 12.8 %collective-permute-start.5 = (bf16[8,128,128]{2,1,0:T(8,128)(2,1)S(1)}, bf16[8,128,128]{2,1,0:T(8,128)(2,1)S(1)}, u32[]{:S(2)}, u32[]{:S(2)}) collective-permute-start(bf16[8,128,128]{2,1,0:T(8,128)(2,1)S(1)} %copy-done.1), channel_id=1, source_target_pairs={{0,32},{32,64},{64,96},{96,0},{1,33},{33,65},{65,97},{97,1},{2,34}... | collective-permute-start | bytes 786440 | tf_op jit(solution)/shard_map/ppermute | solution.py:48
  20.0 12.4 %collective-permute-start.4 = (bf16[8,128,128]{2,1,0:T(8,128)(2,1)S(1)}, bf16[8,128,128]{2,1,0:T(8,128)(2,1)S(1)}, u32[]{:S(2)}, u32[]{:S(2)}) collective-permute-start(bf16[8,128,128]{2,1,0:T(8,128)(2,1)S(1)} %copy-done.1), channel_id=1, source_target_pairs={{0,96},{32,0},{64,32},{96,64},{1,97},{33,1},{65,33},{97,65},{2,98}... | collective-permute-start | bytes 786440 | tf_op jit(solution)/shard_map/ppermute | solution.py:48
  33.2 9.9 %collective-permute-start.8 = (bf16[8,128,128]{2,1,0:T(8,128)(2,1)S(1)}, bf16[8,128,128]{2,1,0:T(8,128)(2,1)S(1)}, u32[]{:S(2)}, u32[]{:S(2)}) collective-permute-start(bf16[8,128,128]{2,1,0:T(8,128)(2,1)S(1)} %collective-permute-done.3.refs_2_.q3), channel_id=1, source_target_pairs={{0,32},{32,64},{64,96},{96,0},{1,33},{33,65},{65,97},{97,1},{2,34}... | collective-permute-start | bytes 786440 | tf_op jit(solution)/shard_map/ppermute | solution.py:48
  34.3 8.9 %collective-permute-start.9 = (bf16[8,128,128]{2,1,0:T(8,128)(2,1)S(1)}, bf16[8,128,128]{2,1,0:T(8,128)(2,1)S(1)}, u32[]{:S(2)}, u32[]{:S(2)}) collective-permute-start(bf16[8,128,128]{2,1,0:T(8,128)(2,1)S(1)} %collective-permute-done.4.refs_4_.g1), channel_id=1, source_target_pairs={{0,96},{32,0},{64,32},{96,64},{1,97},{33,1},{65,33},{97,65},{2,98}... | collective-permute-start | bytes 786440 | tf_op jit(solution)/shard_map/ppermute | solution.py:48
  46.1 5.8 %collective-permute-start.12 = (f32[3,32,128]{2,1,0:T(8,128)S(1)}, f32[3,32,128]{2,1,0:T(8,128)S(1)}, u32[]{:S(2)}, u32[]{:S(2)}) collective-permute-start(f32[3,32,128]{2,1,0:T(8,128)S(1)} %forward.3.s0), channel_id=1, source_target_pairs={{0,96},{32,0},{64,32},{96,64},{1,97},{33,1},{65,33},{97,65},{2,98}... | collective-permute-start | bytes 147464 | tf_op jit(solution)/shard_map/ppermute | solution.py:48
  50.1 5.7 %collective-permute-start.11 = (f32[3,32,128]{2,1,0:T(8,128)S(1)}, f32[3,32,128]{2,1,0:T(8,128)S(1)}, u32[]{:S(2)}, u32[]{:S(2)}) collective-permute-start(f32[3,32,128]{2,1,0:T(8,128)S(1)} %forward.3.s0), channel_id=1, source_target_pairs={{0,64},{32,96},{64,0},{96,32},{1,65},{33,97},{65,1},{97,33},{2,66}... | collective-permute-start | bytes 147464 | tf_op jit(solution)/shard_map/ppermute | solution.py:48
  50.1 5.8 %collective-permute-start.10 = (f32[3,32,128]{2,1,0:T(8,128)S(1)}, f32[3,32,128]{2,1,0:T(8,128)S(1)}, u32[]{:S(2)}, u32[]{:S(2)}) collective-permute-start(f32[3,32,128]{2,1,0:T(8,128)S(1)} %forward.3.s0), channel_id=1, source_target_pairs={{0,32},{32,64},{64,96},{96,0},{1,33},{33,65},{65,97},{97,1},{2,34}... | collective-permute-start | bytes 147464 | tf_op jit(solution)/shard_map/ppermute | solution.py:48
  72.4 24.2 %all-to-all-start.1 = ((bf16[16,256,128]{2,1,0:T(8,128)(2,1)}), bf16[16,256,128]{2,1,0:T(8,128)(2,1)S(1)}, u32[]{:S(2)}, u32[]{:S(2)}) async-start(bf16[16,256,128]{2,1,0:T(8,128)(2,1)} %add_convert_fusion), calls=%async_computation.1 | async-start | bytes 2097152 | tf_op jit(solution)/shard_map/all_to_all | solution.py:57
  78.6 21.8 %collective-permute-start.13 = (bf16[8,128,128]{2,1,0:T(8,128)(2,1)}, bf16[8,128,128]{2,1,0:T(8,128)(2,1)S(1)}, u32[]{:S(2)}, u32[]{:S(2)}) collective-permute-start(bf16[8,128,128]{2,1,0:T(8,128)(2,1)} %get-tuple-element.43), channel_id=1, source_target_pairs={{0,32},{32,64},{64,96},{96,0},{1,33},{33,65},{65,97},{97,1},{2,34}... | collective-permute-start | bytes 786440 | tf_op jit(solution)/shard_map/ppermute | solution.py:48
  78.6 21.7 %collective-permute-start.14 = (bf16[8,128,128]{2,1,0:T(8,128)(2,1)}, bf16[8,128,128]{2,1,0:T(8,128)(2,1)S(1)}, u32[]{:S(2)}, u32[]{:S(2)}) collective-permute-start(bf16[8,128,128]{2,1,0:T(8,128)(2,1)} %get-tuple-element.44), channel_id=1, source_target_pairs={{0,96},{32,0},{64,32},{96,64},{1,97},{33,1},{65,33},{97,65},{2,98}... | collective-permute-start | bytes 786440 | tf_op jit(solution)/shard_map/ppermute | solution.py:48
  81.9 18.5 %collective-permute-start.15 = (bf16[8,128,128]{2,1,0:T(8,128)(2,1)}, bf16[8,128,128]{2,1,0:T(8,128)(2,1)S(1)}, u32[]{:S(2)}, u32[]{:S(2)}) collective-permute-start(bf16[8,128,128]{2,1,0:T(8,128)(2,1)} %get-tuple-element.45), channel_id=1, source_target_pairs={{0,64},{32,96},{64,0},{96,32},{1,65},{33,97},{65,1},{97,33},{2,66}... | collective-permute-start | bytes 786440 | tf_op jit(solution)/shard_map/ppermute | solution.py:48
  97.0 16.1 %collective-permute-start.18 = (bf16[128,2048]{1,0:T(8,128)(2,1)S(1)}, bf16[128,2048]{1,0:T(8,128)(2,1)S(1)}, u32[]{:S(2)}, u32[]{:S(2)}) collective-permute-start(bf16[128,2048]{1,0:T(8,128)(2,1)S(1)} %bitcast.21), channel_id=1, source_target_pairs={{0,32},{32,64},{64,96},{96,0},{1,33},{33,65},{65,97},{97,1},{2,34}... | collective-permute-start | bytes 1572872 | tf_op jit(solution)/shard_map/ppermute | solution.py:48
  97.1 17.1 %collective-permute-start.19 = (bf16[128,2048]{1,0:T(8,128)(2,1)S(1)}, bf16[128,2048]{1,0:T(8,128)(2,1)S(1)}, u32[]{:S(2)}, u32[]{:S(2)}) collective-permute-start(bf16[128,2048]{1,0:T(8,128)(2,1)S(1)} %bitcast.18), channel_id=1, source_target_pairs={{0,96},{32,0},{64,32},{96,64},{1,97},{33,1},{65,33},{97,65},{2,98}... | collective-permute-start | bytes 1572872 | tf_op jit(solution)/shard_map/ppermute | solution.py:48
  100.5 25.0 %collective-permute-start.23 = (bf16[128,2048]{1,0:T(8,128)(2,1)S(1)}, bf16[128,2048]{1,0:T(8,128)(2,1)}, u32[]{:S(2)}, u32[]{:S(2)}) collective-permute-start(bf16[128,2048]{1,0:T(8,128)(2,1)S(1)} %bitcast.22), channel_id=1, source_target_pairs={{0,96},{32,0},{64,32},{96,64},{1,97},{33,1},{65,33},{97,65},{2,98}... | collective-permute-start | bytes 1572872 | tf_op jit(solution)/shard_map/ppermute | solution.py:48
  102.3 23.3 %collective-permute-start.22 = (bf16[128,2048]{1,0:T(8,128)(2,1)S(1)}, bf16[128,2048]{1,0:T(8,128)(2,1)}, u32[]{:S(2)}, u32[]{:S(2)}) collective-permute-start(bf16[128,2048]{1,0:T(8,128)(2,1)S(1)} %bitcast.19), channel_id=1, source_target_pairs={{0,32},{32,64},{64,96},{96,0},{1,33},{33,65},{65,97},{97,1},{2,34}... | collective-permute-start | bytes 1572872 | tf_op jit(solution)/shard_map/ppermute | solution.py:48
  114.2 14.3 %all-to-all-start.2 = ((bf16[16,64,128]{2,1,0:T(8,128)(2,1)}), bf16[16,64,128]{2,1,0:T(8,128)(2,1)S(1)}, u32[]{:S(2)}, u32[]{:S(2)}) async-start(bf16[16,64,128]{2,1,0:T(8,128)(2,1)} %maximum_select_fusion), calls=%async_computation.2 | async-start | bytes 524288 | tf_op jit(solution)/shard_map/all_to_all | solution.py:57
  117.8 14.7 %collective-permute-start.20 = (bf16[128,2048]{1,0:T(8,128)(2,1)S(1)}, bf16[128,2048]{1,0:T(8,128)(2,1)S(1)}, u32[]{:S(2)}, u32[]{:S(2)}) collective-permute-start(bf16[128,2048]{1,0:T(8,128)(2,1)S(1)} %collective-permute-done.19.k1), channel_id=1, source_target_pairs={{0,96},{32,0},{64,32},{96,64},{1,97},{33,1},{65,33},{97,65},{2,98}... | collective-permute-start | bytes 1572872 | tf_op jit(solution)/shard_map/ppermute | solution.py:48
  120.0 12.4 %collective-permute-start.21 = (bf16[128,2048]{1,0:T(8,128)(2,1)S(1)}, bf16[128,2048]{1,0:T(8,128)(2,1)S(1)}, u32[]{:S(2)}, u32[]{:S(2)}) collective-permute-start(bf16[128,2048]{1,0:T(8,128)(2,1)S(1)} %collective-permute-done.18.v3), channel_id=1, source_target_pairs={{0,32},{32,64},{64,96},{96,0},{1,33},{33,65},{65,97},{97,1},{2,34}... | collective-permute-start | bytes 1572872 | tf_op jit(solution)/shard_map/ppermute | solution.py:48
  (7 other events, 51.6 us)
